TPU v7x, 32 devices: a whole 2x2x4 slice. The times are simulated.
32 devices in a mesh: blk: 8 (over z, x), batch: 4 (over y, core).
Axes of the slice: x: 2, y: 2, z: 4, core: 2. Of those that a mesh axis runs over, the one named last changes fastest.
Arguments:
- queries: bfloat16 [4, 2048, 2048], P('batch', 'blk'), may hold values from -8 to 8
- keys: bfloat16 [4, 2048, 1024], P('batch', 'blk'), may hold values from -8 to 8
- values: bfloat16 [4, 2048, 1024], P('batch', 'blk'), may hold values from -6 to 6
- seg_ids: int32 [4, 2048], P('batch', 'blk'), may hold values from 0 to 6, as said below
- lengths: int32 [4, 7], P('batch'), may hold values from 32 to 512, as said below
- live: int32 [4, 8, 2], P('batch', 'blk'), may hold values from 0 to 1, as said below
- page_table: int32 [4, 7, 2], replicated, may hold values from 0 to 31, as said below
- pool: bfloat16 [32, 16, 2048], P('batch'), may hold values from -6 to 6
Outputs:
- attended: bfloat16 [4, 2048, 2048], P('batch', 'blk')
- cache_keys: bfloat16 [4, 2048, 1024], P('batch', 'blk')
Inputs may be any that keep to these rules, and one draw needn't show every extreme that they name: Each stream's lengths sum to 2048; one of them is exactly 512, three lie between 384 and 480, and three between 32 and 128, in random order. seg_ids[b, t] is the prompt that token t falls in under lengths[b]: it never decreases and every prompt number appears. live[b, j, r - 1] is 1 exactly when j >= r and the first token of block j and the last token of block j - r have the same seg_ids. `page_table`: page p is held by index p // 8 of batch. Of one stream's 7 * 2 pages, at most 5 are held by any one index of batch, and exactly 5 by one of them in every stream.
All inputs are finite; a program needn't handle non-finite values.
Results may differ from a plain program's by a relative error of at most 0.0055.
The roundings to bfloat16 on the way count: a program that leaves them out, or rounds other values in their place, can miss the bound.
Values may be sent and summed in bfloat16 or wider, within the bound.
No kernel may reach another device: no remote copies, remote signals or barrier semaphores. Data moves between devices by JAX's collectives and lax.ppermute only.
A program may use at most 128 MiB of HBM per device.

v0:
```python
import math

import jax
import jax.numpy as jnp
import numpy as np
from jax import lax
from jax.experimental import pallas as pl
from jax.experimental.pallas import tpu as pltpu
from jax.sharding import PartitionSpec as P

QUERY_HEADS = 16
KEY_VALUE_HEADS = 8
HEAD_SIZE = 128
GROUP = QUERY_HEADS // KEY_VALUE_HEADS
HALF = HEAD_SIZE // 2
ROPE_BASE = 1000000.0
HIDDEN = -1e30
LANES = 128
ROW_TILE = 64
SOFTMAX_TILE = 16
HEADS_PER_STEP = 2
PREPARE_STEPS = 2


def cost(flops):
    return pl.CostEstimate(flops=flops, bytes_accessed=0, transcendentals=0)


TABLES_COST = cost(2_000_000_000)
PREPARE_COST = cost(0)
OWN_COST = cost(0)
JOIN_COST = cost(0)
GATHER_COST = cost(0)
EXP2_SCALE = math.log2(math.e) / math.sqrt(HEAD_SIZE)

FREQ_POWERS = [float(ROPE_BASE ** (-(2**k) / HALF)) for k in range(HALF.bit_length() - 1)]

PIO2_A = float(np.float32(1.5703125))
PIO2_B = float(np.float32(4.837512969970703125e-4))
PIO2_C = float(np.float32(math.pi / 2 - 1.5703125 - 4.837512969970703125e-4))


def shifted(value, steps):
    count = lax.axis_size("blk")
    return lax.ppermute(value, "blk", [(source, source + steps) for source in range(count - steps)])


def padded_keys(count):
    return -(-count // LANES) * LANES


def vmem_bytes(key_count):
    return 16 * 1024 * (1024 + key_count)


def sine_cosine(angle):
    turns = jnp.floor(angle * (2.0 / math.pi) + 0.5)
    rest = ((angle - turns * PIO2_A) - turns * PIO2_B) - turns * PIO2_C
    square = rest * rest
    sine = rest + rest * square * (
        -1.6666654611e-1 + square * (8.3321608736e-3 - square * 1.9515295891e-4)
    )
    cosine = 1.0 - 0.5 * square + square * square * (
        4.166664568298827e-2 + square * (-1.388731625493765e-3 + square * 2.443315711809948e-5)
    )
    quadrant = turns.astype(jnp.int32) & 3
    swapped = (quadrant & 1) == 1
    sine_out = jnp.where(swapped, cosine, sine)
    cosine_out = jnp.where(swapped, sine, cosine)
    sine_out = jnp.where(quadrant >= 2, -sine_out, sine_out)
    cosine_out = jnp.where((quadrant == 1) | (quadrant == 2), -cosine_out, cosine_out)
    return sine_out, cosine_out


def rotate(head, cosine, signed_sine):
    wide = head.astype(jnp.float32)
    return (wide * cosine + pltpu.roll(wide, HALF, 1) * signed_sine).astype(jnp.bfloat16)


def tables_kernel(
    rows, steps, segs, prefix_len, table_shape, integers_ref,
    page_out, cos_own, sin_own, cos_last, sin_last, cos_far, sin_far, own_bias, last_bias, far_bias,
):
    block_start = lax.axis_index("blk") * rows
    starts = [jnp.int32(0)]
    for seg in range(1, segs):
        starts.append(starts[-1] + integers_ref[seg - 1])
    lane = lax.broadcasted_iota(jnp.int32, (ROW_TILE, LANES), 1)
    row = lax.broadcasted_iota(jnp.int32, (ROW_TILE, LANES), 0)
    freq = jnp.ones((ROW_TILE, LANES), jnp.float32)
    for bit, power in enumerate(FREQ_POWERS):
        freq = jnp.where((lane >> bit) & 1 == 1, freq * power, freq)
    column = lax.axis_index("batch")
    seg_pages = table_shape[2]
    first = segs + steps + column * segs * seg_pages
    for page in range(segs * seg_pages):
        seg, place = divmod(page, seg_pages)
        page_out[page] = integers_ref[first + place * segs + seg]
    for step in range(steps + 1):
        for tile in range(0, rows, ROW_TILE):
            index = block_start + (tile - step * rows) + row
            own_start = jnp.zeros(index.shape, jnp.int32)
            for seg in range(1, segs):
                own_start = jnp.where(index >= starts[seg], starts[seg], own_start)
            place = (prefix_len + index - own_start).astype(jnp.float32)
            sine, cosine = sine_cosine(place * freq)
            sine = jnp.where(lane < HALF, -sine, sine)
            cos_out, sin_out = ((cos_own, sin_own), (cos_last, sin_last), (cos_far, sin_far))[
                min(step, 2)
            ]
            span = pl.ds(max(step - 2, 0) * rows + tile, ROW_TILE)
            cos_out[span, :] = cosine
            sin_out[span, :] = sine
    for tile in range(0, rows, ROW_TILE):
        span = pl.ds(tile, ROW_TILE)
        query_index = block_start + tile + row
        own_start = jnp.zeros(query_index.shape, jnp.int32)
        first_page_token = jnp.zeros(query_index.shape, jnp.int32)
        for seg in range(1, segs):
            later = query_index >= starts[seg]
            own_start = jnp.where(later, starts[seg], own_start)
            first_page_token = jnp.where(later, seg * prefix_len, first_page_token)
        for step in range(steps + 1):
            limit = query_index
            if step > 0:
                limit = jnp.where(integers_ref[segs + step - 1] > 0, limit, -1)
            for column in range(0, rows, LANES):
                key_index = block_start + (column - step * rows) + lane
                seen = (key_index >= own_start) & (key_index <= limit)
                bias = jnp.where(seen, 0.0, HIDDEN)
                if step == 0:
                    own_bias[span, pl.ds(column, LANES)] = bias
                elif step == 1:
                    last_bias[span, pl.ds(column, LANES)] = bias
                else:
                    far_bias[span, pl.ds((step - 2) * rows + column, LANES)] = bias
        base = (steps - 1) * rows
        for column in range(0, far_bias.shape[1] - base, LANES):
            offset = column + lane - first_page_token
            seen = (offset >= 0) & (offset < prefix_len)
            far_bias[span, pl.ds(base + column, LANES)] = jnp.where(seen, 0.0, HIDDEN)


def tables(rows, pool_page, integers, segs, steps, table_shape):
    prefix_len = table_shape[2] * pool_page
    pages = table_shape[1] * table_shape[2]
    far_rows = (steps - 1) * rows
    far_keys = padded_keys(far_rows + segs * prefix_len)
    block = jax.ShapeDtypeStruct((rows, HEAD_SIZE), jnp.float32)
    far = jax.ShapeDtypeStruct((far_rows, HEAD_SIZE), jnp.float32)
    shapes = [
        jax.ShapeDtypeStruct((pages,), jnp.int32),
        *[block] * 4,
        far,
        far,
        *[jax.ShapeDtypeStruct((rows, rows), jnp.float32)] * 2,
        jax.ShapeDtypeStruct((rows, far_keys), jnp.float32),
    ]
    return pl.pallas_call(
        lambda *refs: tables_kernel(rows, steps, segs, prefix_len, table_shape, *refs),
        in_specs=[pl.BlockSpec(memory_space=pltpu.SMEM)],
        out_specs=[pl.BlockSpec(memory_space=pltpu.SMEM)]
        + [pl.BlockSpec(memory_space=pltpu.VMEM)] * (len(shapes) - 1),
        out_shape=shapes,
        compiler_params=pltpu.CompilerParams(vmem_limit_bytes=vmem_bytes(far_keys + far_rows)),
        cost_estimate=TABLES_COST,
        name="tables",
    )(integers)


def prepare_kernel(
    rows, cos_own, sin_own, q_ref, k_ref, v_ref, pool_ref, q_out, k_out, k_copy, v_copy, pool_copy
):
    for tile in range(0, rows, ROW_TILE):
        span = pl.ds(tile, ROW_TILE)
        cosine = cos_own[span, :]
        signed_sine = sin_own[span, :]
        for source, target in ((q_ref, q_out), (k_ref, k_out)):
            for start in range(0, source.shape[2], HEAD_SIZE):
                columns = pl.ds(start, HEAD_SIZE)
                turned = rotate(source[0, span, columns], cosine, signed_sine)
                target[0, span, columns] = turned
                if source is k_ref:
                    k_copy[0, span, columns] = turned
    v_copy[...] = v_ref[...]
    pool_copy[...] = pool_ref[...]


def prepare(cosine, signed_sine, queries, keys, values, pool):
    rows = queries.shape[1]
    whole = lambda part: (0, 0)
    by_part = lambda part: (0, 0, part)
    wide = pl.BlockSpec((1, rows, queries.shape[2] // PREPARE_STEPS), by_part)
    narrow = pl.BlockSpec((1, rows, keys.shape[2] // PREPARE_STEPS), by_part)
    some_pages = pl.BlockSpec(
        (pool.shape[0] // PREPARE_STEPS, *pool.shape[1:]), lambda part: (part, 0, 0)
    )
    table = pl.BlockSpec(cosine.shape, whole)
    return pl.pallas_call(
        lambda *refs: prepare_kernel(rows, *refs),
        grid=(PREPARE_STEPS,),
        in_specs=[table, table, wide, narrow, narrow, some_pages],
        out_specs=[wide, narrow, narrow, narrow, some_pages],
        out_shape=[
            jax.ShapeDtypeStruct(array.shape, array.dtype)
            for array in (queries, keys, keys, values, pool)
        ],
        compiler_params=pltpu.CompilerParams(vmem_limit_bytes=vmem_bytes(rows)),
        cost_estimate=PREPARE_COST,
        name="prepare",
    )(cosine, signed_sine, queries, keys, values, pool)


def stacked_queries(q_ref, part):
    return jnp.concatenate(
        [q_ref[0, :, pl.ds((part * GROUP + h) * HEAD_SIZE, HEAD_SIZE)] for h in range(GROUP)],
        axis=0,
    )


def rotate_rows(target, first, source, lanes, cos_ref, sin_ref):
    rows = source.shape[1]
    for tile in range(0, rows, ROW_TILE):
        span = pl.ds(first + tile, ROW_TILE)
        target[span, :] = rotate(
            source[0, pl.ds(tile, ROW_TILE), lanes], cos_ref[span, :], sin_ref[span, :]
        )


def own_kernel(rows, bias_ref, q_ref, k_ref, v_ref, mean_ref, level_ref, *work):
    k_parts, v_parts, scores, weights, tops = split_work(work)
    group = pl.program_id(0)

    @pl.when(group == 0)
    def _():
        fill_ones(v_parts)
        level_ref[...] = jnp.zeros(level_ref.shape, jnp.float32)

    for part in range(HEADS_PER_STEP):
        lanes = pl.ds(part * HEAD_SIZE, HEAD_SIZE)
        k_parts[part][...] = k_ref[0, :, lanes]
        v_parts[part][:, pl.ds(0, HEAD_SIZE)] = v_ref[0, :, lanes]

    for part in range(HEADS_PER_STEP):
        score_part(part, q_ref, k_parts, scores)
    lane = lax.broadcasted_iota(jnp.int32, (rows, LANES), 1)
    for part in range(HEADS_PER_STEP):
        for start in range(0, GROUP * rows, SOFTMAX_TILE):
            span = pl.ds(start, SOFTMAX_TILE)
            bias = bias_ref[pl.ds(start % rows, SOFTMAX_TILE), :]
            score = scores[part][span, :] * EXP2_SCALE + bias
            highest = jnp.max(score, axis=1, keepdims=True)
            weights[part][span, :] = jnp.exp2(score - highest).astype(jnp.bfloat16)
            tops[part][span, :] = jnp.broadcast_to(highest, (SOFTMAX_TILE, LANES))
        summed = jnp.dot(weights[part][...], v_parts[part][...], preferred_element_type=jnp.float32)
        total = summed[:, HEAD_SIZE:]
        store_part(part, group, rows, lane, summed[:, :HEAD_SIZE] / total,
                   tops[part][...] + jnp.log2(total), mean_ref, level_ref)


def fill_ones(v_parts):
    for v_all in v_parts:
        v_all[:, pl.ds(HEAD_SIZE, HEAD_SIZE)] = jnp.ones((v_all.shape[0], HEAD_SIZE), jnp.bfloat16)


def split_work(work):
    return [work[i : i + HEADS_PER_STEP] for i in range(0, len(work), HEADS_PER_STEP)]


def score_part(part, q_ref, k_parts, scores):
    scores[part][...] = lax.dot_general(
        stacked_queries(q_ref, part), k_parts[part][...], (((1,), (1,)), ((), ())),
        preferred_element_type=jnp.float32,
    )


def store_part(part, group, rows, lane, mean, level, mean_ref, level_ref):
    for h in range(GROUP):
        own = part * GROUP + h
        span = slice(h * rows, (h + 1) * rows)
        mean_ref[:, pl.ds(own * HEAD_SIZE, HEAD_SIZE)] = mean[span]
        head = group * (HEADS_PER_STEP * GROUP) + own
        level_ref[...] = jnp.where(lane == head, level[span], level_ref[...])


def work_shapes(rows, key_count):
    shapes = [
        pltpu.VMEM((key_count, HEAD_SIZE), jnp.bfloat16),
        pltpu.VMEM((key_count, 2 * HEAD_SIZE), jnp.bfloat16),
        pltpu.VMEM((GROUP * rows, key_count), jnp.float32),
        pltpu.VMEM((GROUP * rows, key_count), jnp.bfloat16),
        pltpu.VMEM((GROUP * rows, LANES), jnp.float32),
    ]
    return [shape for shape in shapes for _ in range(HEADS_PER_STEP)]


def attend_own(bias, query, key, value):
    rows, q_width = query.shape[1:]
    by_group = lambda group: (0, 0, group)
    narrow = pl.BlockSpec((1, rows, HEADS_PER_STEP * HEAD_SIZE), by_group)
    wide = HEADS_PER_STEP * GROUP * HEAD_SIZE
    return pl.pallas_call(
        lambda *refs: own_kernel(rows, *refs),
        grid=(KEY_VALUE_HEADS // HEADS_PER_STEP,),
        in_specs=[
            pl.BlockSpec(bias.shape, lambda group: (0, 0)),
            pl.BlockSpec((1, rows, wide), by_group),
            narrow,
            narrow,
        ],
        out_specs=[
            pl.BlockSpec((rows, wide), lambda group: (0, group)),
            pl.BlockSpec((rows, LANES), lambda group: (0, 0)),
        ],
        out_shape=[
            jax.ShapeDtypeStruct((rows, q_width), jnp.float32),
            jax.ShapeDtypeStruct((rows, LANES), jnp.float32),
        ],
        scratch_shapes=work_shapes(rows, rows),
        compiler_params=pltpu.CompilerParams(vmem_limit_bytes=vmem_bytes(rows)),
        cost_estimate=OWN_COST,
        name="own",
    )(bias, query, key, value)


def gather_kernel(pool_rows, places, table_ref, *refs):
    *shards, paged, sem = refs
    column = lax.axis_index("batch")

    def copy(shard, place, page):
        return pltpu.make_async_copy(shard.at[place], paged.at[page], sem.at[page])

    for page in range(paged.shape[0]):
        number = table_ref[page]
        apart = lax.div(number, jnp.int32(pool_rows)) ^ column
        place = lax.rem(number, jnp.int32(pool_rows))
        for (which, first), shard in zip(places, shards):
            inside = place - first

            @pl.when((apart == which) & (inside >= 0) & (inside < shard.shape[0]))
            def _(shard=shard, inside=inside, page=page):
                copy(shard, inside, page).start()

    for page in range(paged.shape[0]):
        copy(shards[0], 0, page).wait()


def gather_pages(numbers, found):
    places, shards = [shard[:2] for shard in found], [shard[2] for shard in found]
    pool_rows = shards[0].shape[0]
    return pl.pallas_call(
        lambda *refs: gather_kernel(pool_rows, places, *refs),
        in_specs=[pl.BlockSpec(memory_space=pltpu.SMEM)]
        + [pl.BlockSpec(memory_space=pl.ANY)] * len(shards),
        out_specs=pl.BlockSpec(memory_space=pltpu.VMEM),
        out_shape=jax.ShapeDtypeStruct(numbers.shape + shards[0].shape[1:], jnp.bfloat16),
        scratch_shapes=[pltpu.SemaphoreType.DMA(numbers.shape)],
        compiler_params=pltpu.CompilerParams(vmem_limit_bytes=vmem_bytes(0)),
        cost_estimate=GATHER_COST,
        name="gather",
    )(numbers, *shards)


def join_heads(
    final, group, rows, k_parts, v_parts, scores, weights, tops,
    bias_ref, level_ref, mean_ref, q_ref, out_ref, level_out,
):
    for part in range(HEADS_PER_STEP):
        score_part(part, q_ref, k_parts, scores)
    lane = lax.broadcasted_iota(jnp.int32, (SOFTMAX_TILE, LANES), 1)
    wide_lane = lax.broadcasted_iota(jnp.int32, (rows, LANES), 1)
    for part in range(HEADS_PER_STEP):
        for start in range(0, GROUP * rows, SOFTMAX_TILE):
            span = pl.ds(start, SOFTMAX_TILE)
            row_span = pl.ds(start % rows, SOFTMAX_TILE)
            head = group * (HEADS_PER_STEP * GROUP) + part * GROUP + start // rows
            score = scores[part][span, :] * EXP2_SCALE + bias_ref[row_span, :]
            level = jnp.sum(
                jnp.where(lane == head, level_ref[row_span, :], 0.0), axis=1, keepdims=True
            )
            highest = jnp.maximum(jnp.max(score, axis=1, keepdims=True), level)
            weights[part][span, :] = jnp.exp2(score - highest).astype(jnp.bfloat16)
            if final:
                shrink = jnp.exp2(level - highest)
                tops[part][span, :] = jnp.broadcast_to(shrink, (SOFTMAX_TILE, LANES))
            else:
                tops[part][span, :] = jnp.where(lane < HALF, highest, level)
        summed = jnp.dot(weights[part][...], v_parts[part][...], preferred_element_type=jnp.float32)
        if final:
            shrink = tops[part][...]
        else:
            both = tops[part][...]
            turned = pltpu.roll(both, HALF, 1)
            low = lax.broadcasted_iota(jnp.int32, both.shape, 1) < HALF
            highest = jnp.where(low, both, turned)
            shrink = jnp.exp2(jnp.where(low, turned, both) - highest)
        total = summed[:, HEAD_SIZE:] + shrink
        before = jnp.concatenate(
            [mean_ref[:, pl.ds((part * GROUP + h) * HEAD_SIZE, HEAD_SIZE)] for h in range(GROUP)],
            axis=0,
        )
        mean = (before * shrink + summed[:, :HEAD_SIZE]) / total
        if final:
            for h in range(GROUP):
                lanes = pl.ds((part * GROUP + h) * HEAD_SIZE, HEAD_SIZE)
                out_ref[0, :, lanes] = mean[h * rows : (h + 1) * rows].astype(jnp.bfloat16)
        else:
            level = highest + jnp.log2(total)
            store_part(part, group, rows, wide_lane, mean, level, out_ref, level_out)


def far_kernel(
    rows, blocks, cos_ref, sin_ref, bias_ref, level_ref, mean_ref, q_ref, page_keys, page_values, *refs
):
    keys, values, refs = refs[:blocks], refs[blocks : 2 * blocks], refs[2 * blocks :]
    mean_out, level_out = refs[:2]
    work = split_work(refs[2:])
    k_parts, v_parts = work[:2]
    group = pl.program_id(0)
    prefix_rows = page_keys.shape[0] * page_keys.shape[1]
    base = blocks * rows

    @pl.when(group == 0)
    def _():
        fill_ones(v_parts)
        level_out[...] = jnp.zeros(level_out.shape, jnp.float32)
        rest = k_parts[0].shape[0] - base - prefix_rows
        if rest:
            blank = jnp.zeros((rest, HEAD_SIZE), jnp.bfloat16)
            for k_all, v_all in zip(k_parts, v_parts):
                k_all[pl.ds(base + prefix_rows, rest), :] = blank
                v_all[pl.ds(base + prefix_rows, rest), pl.ds(0, HEAD_SIZE)] = blank

    for part in range(HEADS_PER_STEP):
        lanes = pl.ds(part * HEAD_SIZE, HEAD_SIZE)
        for block in range(blocks):
            rotate_rows(k_parts[part], block * rows, keys[block], lanes, cos_ref, sin_ref)
            span = pl.ds(block * rows, rows)
            v_parts[part][span, pl.ds(0, HEAD_SIZE)] = values[block][0, :, lanes]
        span = pl.ds(base, prefix_rows)
        k_parts[part][span, :] = page_keys[:, :, lanes].reshape(prefix_rows, HEAD_SIZE)
        v_parts[part][span, pl.ds(0, HEAD_SIZE)] = page_values[:, :, lanes].reshape(
            prefix_rows, HEAD_SIZE
        )
    join_heads(
        False, group, rows, *work, bias_ref, level_ref, mean_ref, q_ref, mean_out, level_out
    )


def last_kernel(
    rows, cos_ref, sin_ref, bias_ref, level_ref, mean_ref, q_ref, key_ref, swapped_value,
    passed_value, direct_value, out_ref, *refs,
):
    work = split_work(refs)
    k_parts, v_parts = work[:2]
    group = pl.program_id(0)
    even = lax.rem(lax.axis_index("blk"), 2) == 0

    @pl.when(group == 0)
    def _():
        fill_ones(v_parts)

    for part in range(HEADS_PER_STEP):
        lanes = pl.ds(part * HEAD_SIZE, HEAD_SIZE)
        rotate_rows(k_parts[part], 0, key_ref, lanes, cos_ref, sin_ref)
        start = 0
        for arrived in (passed_value, direct_value):
            span = pl.ds(start, arrived.shape[1])
            v_parts[part][span, pl.ds(0, HEAD_SIZE)] = jnp.where(
                even, arrived[0, :, lanes], swapped_value[0, span, lanes]
            )
            start += arrived.shape[1]
    join_heads(True, group, rows, *work, bias_ref, level_ref, mean_ref, q_ref, out_ref, None)


def join(cosine, signed_sine, bias, level, mean, query, arrived, pages=None):
    rows = query.shape[1]
    whole = lambda group: (0, 0)
    by_group = lambda group: (0, 0, group)
    width = HEADS_PER_STEP * GROUP * HEAD_SIZE
    wide = pl.BlockSpec((1, rows, width), by_group)
    flat = pl.BlockSpec((rows, width), lambda group: (0, group))
    level_spec = pl.BlockSpec(level.shape, whole)
    table = pl.BlockSpec(cosine.shape, whole)
    in_specs = [table, table, pl.BlockSpec(bias.shape, whole), level_spec, flat, wide]
    arrived_specs = [
        pl.BlockSpec((1, array.shape[1], HEADS_PER_STEP * HEAD_SIZE), by_group)
        for array in arrived
    ]
    operands = [cosine, signed_sine, bias, level, mean, query]
    scratch = work_shapes(rows, bias.shape[1])
    if pages is None:
        kernel = lambda *refs: last_kernel(rows, *refs)
        out_specs, out_shape = wide, jax.ShapeDtypeStruct(query.shape, jnp.bfloat16)
    else:
        kernel = lambda *refs: far_kernel(rows, len(arrived) // 2, *refs)
        groups = KEY_VALUE_HEADS // HEADS_PER_STEP
        for first in (0, groups):
            in_specs.append(
                pl.BlockSpec(
                    (*pages.shape[:2], HEADS_PER_STEP * HEAD_SIZE),
                    lambda group, first=first: (0, 0, first + group),
                )
            )
            operands.append(pages)
        out_specs = [flat, level_spec]
        out_shape = [
            jax.ShapeDtypeStruct(array.shape, jnp.float32) for array in (mean, level)
        ]
    return pl.pallas_call(
        kernel,
        grid=(KEY_VALUE_HEADS // HEADS_PER_STEP,),
        in_specs=in_specs + arrived_specs,
        out_specs=out_specs,
        out_shape=out_shape,
        scratch_shapes=scratch,
        compiler_params=pltpu.CompilerParams(vmem_limit_bytes=vmem_bytes(bias.shape[1])),
        cost_estimate=JOIN_COST,
        name="last" if pages is None else "far",
    )(*operands, *arrived)


def pool_shards(pool, after):
    count = lax.axis_size("batch")

    def swapped(shard, bit):
        return lax.ppermute(shard, "batch", [(c, c ^ bit) for c in range(count)])

    bits = [count >> (step + 1) for step in range(count.bit_length() - 1)]
    shards = {bit: swapped(pool, bit) for bit in bits}
    shards, after = lax.optimization_barrier((shards, after))
    shards = {apart: [shard] for apart, shard in shards.items()}
    for bit in reversed(bits):
        for apart, pieces in list(shards.items()):
            if apart ^ bit not in shards and apart != bit:
                if len(pieces) == 1:
                    middle = pool.shape[0] // 2
                    pieces = [pieces[0][:middle], pieces[0][middle:]]
                shards[apart ^ bit] = [swapped(piece, bit) for piece in pieces]
    found = []
    for apart, pieces in sorted(shards.items()):
        held = pool.shape[0] // len(pieces)
        found += [(apart, place * held, piece) for place, piece in enumerate(pieces)]
    return found


def per_device(queries, keys, values, seg_ids, lengths, live, page_table, pool):
    steps = live.shape[2]
    blocks = lax.axis_size("blk")
    far = [shifted(keys, 2), shifted(values, 2)]
    for step in range(3, steps + 1):
        far += [shifted(keys, step), shifted(values, step)]
    swap = [(j, j ^ 1) for j in range(blocks)]
    even = lax.rem(lax.axis_index("blk"), 2) == 0
    swapped_value = lax.ppermute(values, "blk", swap)
    integers = jnp.concatenate([lengths.ravel(), live.ravel(), jnp.swapaxes(page_table, 1, 2).ravel()])
    (
        table, cos_own, sin_own, cos_last, sin_last, cos_far, sin_far, own_bias, last_bias, far_bias
    ) = tables(keys.shape[1], pool.shape[1], integers, lengths.shape[1], steps, page_table.shape)
    query, key, near_key, near_value, own_shard = prepare(
        cos_own, sin_own, queries, keys, values, pool
    )
    to_swap = jnp.where(even, keys, far[0])
    far_key = lax.ppermute(to_swap, "blk", swap)
    split = values.shape[1] * 3 // 4
    passed_value = lax.ppermute(
        swapped_value[:, :split], "blk", [(j, j + 2) for j in range(0, blocks - 2, 2)]
    )
    mean, level = attend_own(own_bias, query, near_key, near_value)
    shards = pool_shards(pool, (level, to_swap, swapped_value))
    pieces, later_values = lax.optimization_barrier(
        ([shard[2] for shard in shards], values[:, split:])
    )
    shards = [(*shard[:2], piece) for shard, piece in zip(shards, pieces)]
    direct_value = lax.ppermute(
        later_values, "blk", [(j, j + 1) for j in range(1, blocks - 1, 2)]
    )
    mean, level = join(
        cos_far, sin_far, far_bias, level, mean, query, [*far[::2], *far[1::2]],
        pages=gather_pages(table, [(0, 0, own_shard), *shards]),
    )
    result = join(
        cos_last, sin_last, last_bias, level, mean, query,
        [far_key, swapped_value, passed_value, direct_value],
    )
    return (result, key)


def solution(mesh):
    in_specs = (
        P("batch", "blk", None),
        P("batch", "blk", None),
        P("batch", "blk", None),
        P("batch", "blk"),
        P("batch", None),
        P("batch", "blk", None),
        P(),
        P("batch", None, None),
    )
    out_specs = (P("batch", "blk", None), P("batch", "blk", None))
    return jax.shard_map(
        per_device, mesh=mesh, in_specs=in_specs, out_specs=out_specs, check_vma=False
    )
```

profile of v0, /device:TPU:8, one launch (start us, length us, event | category | flops | bytes accessed | tf_op | source)
XLA Modules:
  0.0 40.3 jit_solution(9417481223628162798)
XLA Ops:
  0.6 3.5 %collective-permute-start.2 = (bf16[1,256,1024]{2,1,0:T(8,128)(2,1)}, bf16[1,256,1024]{2,1,0:T(8,128)(2,1)S(1)}, u32[]{:S(2)}, u32[]{:S(2)}) collective-permute-start(bf16[1,256,1024]{2,1,0:T(8,128)(2,1)} %refs_3_.1), channel_id=1, source_target_pairs={{0,8},{4,12},{8,16},{12,20},{16,24},{20,28},{1,9},{5,13},{9,17},{1... | collective-permute-start | bytes 1572872 | tf_op jit(solution)/shard_map/ppermute | solution.py:45
  4.1 0.1 collective-permute-start
  4.2 1.6 %collective-permute-start.1 = (bf16[8,16,2048]{2,1,0:T(8,128)(2,1)}, bf16[8,16,2048]{2,1,0:T(8,128)(2,1)S(1)}, u32[]{:S(2)}, u32[]{:S(2)}) collective-permute-start(bf16[8,16,2048]{2,1,0:T(8,128)(2,1)} %refs_5_.1), channel_id=1, source_target_pairs={{0,2},{1,3},{2,0},{3,1},{4,6},{5,7},{6,4},{7,5},{8,10},{9,11},{10,... | collective-permute-start | bytes 1572872 | tf_op jit(solution)/shard_map/ppermute | solution.py:527
  5.8 1.5 %collective-permute-start.3 = (bf16[1,256,1024]{2,1,0:T(8,128)(2,1)}, bf16[1,256,1024]{2,1,0:T(8,128)(2,1)S(1)}, u32[]{:S(2)}, u32[]{:S(2)}) collective-permute-start(bf16[1,256,1024]{2,1,0:T(8,128)(2,1)} %refs_4_.1), channel_id=1, source_target_pairs={{0,4},{4,0},{8,12},{12,8},{16,20},{20,16},{24,28},{28,24},{1,5},{5... | collective-permute-start | bytes 1572872 | tf_op jit(solution)/shard_map/ppermute | solution.py:555
  7.3 3.5 %collective-permute-start.6 = (bf16[1,256,1024]{2,1,0:T(8,128)(2,1)}, bf16[1,256,1024]{2,1,0:T(8,128)(2,1)S(1)}, u32[]{:S(2)}, u32[]{:S(2)}) collective-permute-start(bf16[1,256,1024]{2,1,0:T(8,128)(2,1)} %refs_4_.1), channel_id=1, source_target_pairs={{0,8},{4,12},{8,16},{12,20},{16,24},{20,28},{1,9},{5,13},{9,17},{1... | collective-permute-start | bytes 1572872 | tf_op jit(solution)/shard_map/ppermute | solution.py:45
  10.8 0.8 %reshape.15 = s32[56]{0:T(128)S(1)} reshape(s32[4,2,7]{2,1,0:T(2,128)} %bitcast.3) | data formatting | bytes 448 | tf_op jit(solution)/shard_map/reshape | solution.py:556
  11.5 0.8 %pad_add_fusion.refs_0_ = s32[65]{0:T(128)S(1)} fusion(s32[56]{0:T(128)S(1)} %reshape.15, s32[2]{0:T(128)} %bitcast.4, s32[7]{0:T(128)} %bitcast.5), kind=kLoop, calls=%fused_computation.1 | loop fusion | flops 130 | bytes 520 | tf_op jit(solution)/shard_map/concatenate | solution.py:556
  12.3 0.0 copy-start
  12.3 0.0 copy-start.1
  12.3 0.0 copy-start.2
  12.3 0.0 copy-start.3
  12.3 2.0 %tables.1 = (s32[14]{0:T(128)S(1)}, f32[256,128]{1,0:T(8,128)S(1)}, f32[256,128]{1,0:T(8,128)S(1)}, f32[256,128]{1,0:T(8,128)S(1)}, f32[256,128]{1,0:T(8,128)S(1...) custom-call(s32[65]{0:T(128)S(1)} %pad_add_fusion.refs_0_), custom_call_target="tpu_custom_call" | custom-call | flops 2000000000 | tf_op jit(solution)/shard_map/tables/pallas_call | solution.py:159
  14.4 0.0 copy-done
  14.4 0.0 copy-done.1
  14.4 0.0 copy-done.2
  14.4 0.0 copy-done.3
  14.4 1.8 %prepare.1 = (bf16[1,256,2048]{2,1,0:T(8,128)(2,1)S(1)}, bf16[1,256,1024]{2,1,0:T(8,128)(2,1)}, bf16[1,256,1024]{2,1,0:T(8,128)(2,1)S(1)}, bf16[1,256,1024]{2,1,0:T(8,128)(2,1)S(1)}, bf16[8,16,2048]{2,1,0:T(8,128)(2,1)S(1)}) custom-call(f32[256,128]{1,0:T(8,128)S(1)} %get-tuple-element.35.refs_0_, f32[256,128]{1,0:T(8,128)S(1)} %get-tuple-element.36.refs_1_, ...), custom_call_target="tpu_custom_call" | custom-call | tf_op jit(solution)/shard_map/prepare/pallas_call | solution.py:199
  16.2 2.8 %own.1 = (f32[256,2048]{1,0:T(8,128)S(1)}, f32[256,128]{1,0:T(8,128)S(1)}) custom-call(f32[256,256]{1,0:T(8,128)S(1)} %get-tuple-element.34.refs_0_, bf16[1,256,2048]{2,1,0:T(8,128)(2,1)S(1)} %get-tuple-element.37.refs_1_.refs_5_, bf16[1,256,1024]{2,1,0:T(8,128)(2,1)S(1)} %get-tuple-element.38.refs_2_, bf16[1,256,1024]{2,1,0:T(8,128)(2,1)S(1)} %get-tuple-element.39.refs_3_), custom_call_target="tpu_custom_call" | custom-call | tf_op jit(solution)/shard_map/own/pallas_call | solution.py:302
  19.0 0.0 collective-permute-done.2.refs_8_
  19.0 0.1 broadcast_select_fusion
  19.1 0.6 %collective-permute-start.7 = (bf16[1,256,1024]{2,1,0:T(8,128)(2,1)S(1)}, bf16[1,256,1024]{2,1,0:T(8,128)(2,1)S(1)}, u32[]{:S(2)}, u32[]{:S(2)}) collective-permute-start(bf16[1,256,1024]{2,1,0:T(8,128)(2,1)S(1)} %broadcast_select_fusion), channel_id=1, source_target_pairs={{0,4},{4,0},{8,12},{12,8},{16,20},{20,16},{24,28},{28,24},{1,5},{5... | collective-permute-start | bytes 1572872 | tf_op jit(solution)/shard_map/ppermute | solution.py:564
  19.7 0.0 collective-permute-done.refs_2_
  19.7 0.0 collective-permute-done.1.refs_3_
  19.7 0.3 collective-permute-done.3.refs_7_
  20.0 0.1 collective-permute-start.4
  20.1 0.5 %collective-permute-start.5 = (bf16[4,16,2048]{2,1,0:T(8,128)(2,1)S(1)}, bf16[4,16,2048]{2,1,0:T(8,128)(2,1)S(1)}, u32[]{:S(2)}, u32[]{:S(2)}) collective-permute-start(bf16[4,16,2048]{2,1,0:T(8,128)(2,1)S(1)} %get-tuple-element.54), channel_id=1, source_target_pairs={{0,1},{1,0},{2,3},{3,2},{4,5},{5,4},{6,7},{7,6},{8,9},{9,8},{10,11... | collective-permute-start | bytes 786440 | tf_op jit(solution)/shard_map/ppermute | solution.py:527
  20.6 3.5 %collective-permute-start.8 = (bf16[1,192,1024]{2,1,0:T(8,128)(2,1)S(1)}, bf16[1,192,1024]{2,1,0:T(8,128)(2,1)S(1)}, u32[]{:S(2)}, u32[]{:S(2)}) collective-permute-start(bf16[1,192,1024]{2,1,0:T(8,128)(2,1)S(1)} %slice.16), channel_id=1, source_target_pairs={{0,8},{8,16},{16,24},{1,9},{9,17},{17,25},{2,10},{10,18},{18,26},{... | collective-permute-start | bytes 1179656 | tf_op jit(solution)/shard_map/ppermute | solution.py:566
  24.1 0.0 collective-permute-done.4.refs_4_
  24.2 0.0 collective-permute-done.5.refs_5_
  24.2 1.3 %collective-permute-start.9 = (bf16[1,64,1024]{2,1,0:T(8,128)(2,1)S(1)}, bf16[1,64,1024]{2,1,0:T(8,128)(2,1)S(1)}, u32[]{:S(2)}, u32[]{:S(2)}) collective-permute-start(bf16[1,64,1024]{2,1,0:T(8,128)(2,1)S(1)} %slice.14), channel_id=1, source_target_pairs={{4,8},{12,16},{20,24},{5,9},{13,17},{21,25},{6,10},{14,18},{22,26}... | collective-permute-start | bytes 393224 | tf_op jit(solution)/shard_map/ppermute | solution.py:575
  25.5 2.4 %gather.1.refs_6_.refs_7_ = bf16[14,16,2048]{2,1,0:T(8,128)(2,1)S(1)} custom-call(s32[14]{0:T(128)S(1)} %get-tuple-element.42.refs_0_, bf16[8,16,2048]{2,1,0:T(8,128)(2,1)S(1)} %get-tuple-element.43.refs_1_, bf16[8,16,2048]{2,1,0:T(8,128)(2,1)S(1)} %collective-permute-done.refs_2_, bf16[8,16,2048]{2,1,0:T(8,128)(2,1)S(1)} %collective-permute-done.1.refs_3_, ...), custom_call_target="tpu_custom_call" | custom-call | tf_op jit(solution)/shard_map/gather/pallas_call | solution.py:351
  27.8 0.9 %collective-permute-done.6.refs_9_ = bf16[1,256,1024]{2,1,0:T(8,128)(2,1)S(1)} collective-permute-done((bf16[1,256,1024]{2,1,0:T(8,128)(2,1)}, bf16[1,256,1024]{2,1,0:T(8,128)(2,1)S(1)}, u32[]{:S(2)}, u32[]{:S(2)}) %collective-permute-start.6) | collective-permute-done | bytes 524320 | tf_op jit(solution)/shard_map/ppermute | solution.py:45
  28.8 5.2 %far.1 = (f32[256,2048]{1,0:T(8,128)S(1)}, f32[256,128]{1,0:T(8,128)S(1)}) custom-call(f32[256,128]{1,0:T(8,128)S(1)} %get-tuple-element.31.refs_0_, f32[256,128]{1,0:T(8,128)S(1)} %get-tuple-element.32.refs_1_, f32[256,512]{1,0:T(8,128)S(1)} %get-tuple-element.33.refs_2_, f32[256,128]{1,0:T(8,128)S(1)} %get-tuple-element.40.refs_3_, ...), custom_call_target="tpu_custom_call" | custom-call | tf_op jit(solution)/shard_map/far/pallas_call | solution.py:510
  34.0 0.0 collective-permute-done.9.refs_9_
  34.0 2.0 %collective-permute-done.8.refs_8_ = bf16[1,192,1024]{2,1,0:T(8,128)(2,1)S(1)} collective-permute-done((bf16[1,192,1024]{2,1,0:T(8,128)(2,1)S(1)}, bf16[1,192,1024]{2,1,0:T(8,128)(2,1)S(1)}, u32[]{:S(2)}, u32[]{:S(2)}) %collective-permute-start.8) | collective-permute-done | bytes 393248 | tf_op jit(solution)/shard_map/ppermute | solution.py:566
  36.1 0.0 collective-permute-done.7.refs_6_
  36.1 4.2 %last.1 = bf16[1,256,2048]{2,1,0:T(8,128)(2,1)} custom-call(f32[256,128]{1,0:T(8,128)S(1)} %get-tuple-element.28.refs_0_, f32[256,128]{1,0:T(8,128)S(1)} %get-tuple-element.29.refs_1_, f32[256,256]{1,0:T(8,128)S(1)} %get-tuple-element.30.refs_2_, f32[256,128]{1,0:T(8,128)S(1)} %get-tuple-element.50.refs_3_, f32[256,2048]{1,0:T(8,128)S(1)} %get-tuple-element.51.refs_4_, ...), custom_call_target="tpu_custom_call" | custom-call | tf_op jit(solution)/shard_map/last/pallas_call | solution.py:510
  (3 shorter events, 0.1 us)
Async XLA Ops:
  0.6 18.4 %collective-permute-start.2 = (bf16[1,256,1024]{2,1,0:T(8,128)(2,1)}, bf16[1,256,1024]{2,1,0:T(8,128)(2,1)S(1)}, u32[]{:S(2)}, u32[]{:S(2)}) collective-permute-start(bf16[1,256,1024]{2,1,0:T(8,128)(2,1)} %refs_3_.1), channel_id=1, source_target_pairs={{0,8},{4,12},{8,16},{12,20},{16,24},{20,28},{1,9},{5,13},{9,17},{1... | collective-permute-start | bytes 1572872 | tf_op jit(solution)/shard_map/ppermute | solution.py:45
  4.1 15.6 %collective-permute-start = (bf16[8,16,2048]{2,1,0:T(8,128)(2,1)}, bf16[8,16,2048]{2,1,0:T(8,128)(2,1)S(1)}, u32[]{:S(2)}, u32[]{:S(2)}) collective-permute-start(bf16[8,16,2048]{2,1,0:T(8,128)(2,1)} %refs_5_.1), channel_id=1, source_target_pairs={{0,1},{1,0},{2,3},{3,2},{4,5},{5,4},{6,7},{7,6},{8,9},{9,8},{10,11... | collective-permute-start | bytes 1572872 | tf_op jit(solution)/shard_map/ppermute | solution.py:527
  4.2 15.5 %collective-permute-start.1 = (bf16[8,16,2048]{2,1,0:T(8,128)(2,1)}, bf16[8,16,2048]{2,1,0:T(8,128)(2,1)S(1)}, u32[]{:S(2)}, u32[]{:S(2)}) collective-permute-start(bf16[8,16,2048]{2,1,0:T(8,128)(2,1)} %refs_5_.1), channel_id=1, source_target_pairs={{0,2},{1,3},{2,0},{3,1},{4,6},{5,7},{6,4},{7,5},{8,10},{9,11},{10,... | collective-permute-start | bytes 1572872 | tf_op jit(solution)/shard_map/ppermute | solution.py:527
  5.8 14.2 %collective-permute-start.3 = (bf16[1,256,1024]{2,1,0:T(8,128)(2,1)}, bf16[1,256,1024]{2,1,0:T(8,128)(2,1)S(1)}, u32[]{:S(2)}, u32[]{:S(2)}) collective-permute-start(bf16[1,256,1024]{2,1,0:T(8,128)(2,1)} %refs_4_.1), channel_id=1, source_target_pairs={{0,4},{4,0},{8,12},{12,8},{16,20},{20,16},{24,28},{28,24},{1,5},{5... | collective-permute-start | bytes 1572872 | tf_op jit(solution)/shard_map/ppermute | solution.py:555
  7.3 21.5 %collective-permute-start.6 = (bf16[1,256,1024]{2,1,0:T(8,128)(2,1)}, bf16[1,256,1024]{2,1,0:T(8,128)(2,1)S(1)}, u32[]{:S(2)}, u32[]{:S(2)}) collective-permute-start(bf16[1,256,1024]{2,1,0:T(8,128)(2,1)} %refs_4_.1), channel_id=1, source_target_pairs={{0,8},{4,12},{8,16},{12,20},{16,24},{20,28},{1,9},{5,13},{9,17},{1... | collective-permute-start | bytes 1572872 | tf_op jit(solution)/shard_map/ppermute | solution.py:45
  12.3 2.1 %copy-start = (bf16[1,256,1024]{2,1,0:T(8,128)(2,1)S(1)}, bf16[1,256,1024]{2,1,0:T(8,128)(2,1)}, u32[]{:S(2)}) copy-start(bf16[1,256,1024]{2,1,0:T(8,128)(2,1)} %refs_3_.1) | copy-start | bytes 1572868
  12.3 2.1 %copy-start.1 = (bf16[1,256,2048]{2,1,0:T(8,128)(2,1)S(1)}, bf16[1,256,2048]{2,1,0:T(8,128)(2,1)}, u32[]{:S(2)}) copy-start(bf16[1,256,2048]{2,1,0:T(8,128)(2,1)} %refs_2_.1) | copy-start | bytes 3145732
  12.3 2.1 %copy-start.2 = (bf16[1,256,1024]{2,1,0:T(8,128)(2,1)S(1)}, bf16[1,256,1024]{2,1,0:T(8,128)(2,1)}, u32[]{:S(2)}) copy-start(bf16[1,256,1024]{2,1,0:T(8,128)(2,1)} %refs_4_.1) | copy-start | bytes 1572868
  12.3 2.1 %copy-start.3 = (bf16[8,16,2048]{2,1,0:T(8,128)(2,1)S(1)}, bf16[8,16,2048]{2,1,0:T(8,128)(2,1)}, u32[]{:S(2)}) copy-start(bf16[8,16,2048]{2,1,0:T(8,128)(2,1)} %refs_5_.1) | copy-start | bytes 1572868
  19.1 17.0 %collective-permute-start.7 = (bf16[1,256,1024]{2,1,0:T(8,128)(2,1)S(1)}, bf16[1,256,1024]{2,1,0:T(8,128)(2,1)S(1)}, u32[]{:S(2)}, u32[]{:S(2)}) collective-permute-start(bf16[1,256,1024]{2,1,0:T(8,128)(2,1)S(1)} %broadcast_select_fusion), channel_id=1, source_target_pairs={{0,4},{4,0},{8,12},{12,8},{16,20},{20,16},{24,28},{28,24},{1,5},{5... | collective-permute-start | bytes 1572872 | tf_op jit(solution)/shard_map/ppermute | solution.py:564
  20.0 4.1 %collective-permute-start.4 = (bf16[4,16,2048]{2,1,0:T(8,128)(2,1)S(1)}, bf16[4,16,2048]{2,1,0:T(8,128)(2,1)S(1)}, u32[]{:S(2)}, u32[]{:S(2)}) collective-permute-start(bf16[4,16,2048]{2,1,0:T(8,128)(2,1)S(1)} %get-tuple-element.55), channel_id=1, source_target_pairs={{0,1},{1,0},{2,3},{3,2},{4,5},{5,4},{6,7},{7,6},{8,9},{9,8},{10,11... | collective-permute-start | bytes 786440 | tf_op jit(solution)/shard_map/ppermute | solution.py:527
  20.1 4.1 %collective-permute-start.5 = (bf16[4,16,2048]{2,1,0:T(8,128)(2,1)S(1)}, bf16[4,16,2048]{2,1,0:T(8,128)(2,1)S(1)}, u32[]{:S(2)}, u32[]{:S(2)}) collective-permute-start(bf16[4,16,2048]{2,1,0:T(8,128)(2,1)S(1)} %get-tuple-element.54), channel_id=1, source_target_pairs={{0,1},{1,0},{2,3},{3,2},{4,5},{5,4},{6,7},{7,6},{8,9},{9,8},{10,11... | collective-permute-start | bytes 786440 | tf_op jit(solution)/shard_map/ppermute | solution.py:527
  20.6 15.4 %collective-permute-start.8 = (bf16[1,192,1024]{2,1,0:T(8,128)(2,1)S(1)}, bf16[1,192,1024]{2,1,0:T(8,128)(2,1)S(1)}, u32[]{:S(2)}, u32[]{:S(2)}) collective-permute-start(bf16[1,192,1024]{2,1,0:T(8,128)(2,1)S(1)} %slice.16), channel_id=1, source_target_pairs={{0,8},{8,16},{16,24},{1,9},{9,17},{17,25},{2,10},{10,18},{18,26},{... | collective-permute-start | bytes 1179656 | tf_op jit(solution)/shard_map/ppermute | solution.py:566
  24.2 9.9 %collective-permute-start.9 = (bf16[1,64,1024]{2,1,0:T(8,128)(2,1)S(1)}, bf16[1,64,1024]{2,1,0:T(8,128)(2,1)S(1)}, u32[]{:S(2)}, u32[]{:S(2)}) collective-permute-start(bf16[1,64,1024]{2,1,0:T(8,128)(2,1)S(1)} %slice.14), channel_id=1, source_target_pairs={{4,8},{12,16},{20,24},{5,9},{13,17},{21,25},{6,10},{14,18},{22,26}... | collective-permute-start | bytes 393224 | tf_op jit(solution)/shard_map/ppermute | solution.py:575
where the time goes:
time: 41.1 us; the launch traced here: 40.3 us
  Pallas kernels  18.5 us (45%)
  starting transfers between devices  16.1 us (39%)
  waiting for transfers between devices  3.26 us (8%)
  local copies, waits for them, and re-layouts  0.86 us (2%)
  other arithmetic  0.82 us (2%)
  between operations  0.81 us (2%)
    pallas_call x2, Pallas kernels, join(): pl.pallas_call(kernel, grid=(KEY_VALUE_HEADS // HEADS_PER_STEP,), in_spec...  9.47 us
    ppermute x2, starting transfers between devices, shifted(): lax.ppermute(value, 'blk', [(source, source + steps) for source in range(...  6.96 us
    ppermute x1, starting transfers between devices, per_device(): lax.ppermute(swapped_value[:, :split], 'blk', [(j, j + 2) for j in range(...  3.48 us
    pallas_call x1, Pallas kernels, attend_own(): pl.pallas_call(lambda *refs: own_kernel(rows, *refs), grid=(KEY_VALUE_HEA...  2.79 us
    pallas_call x1, Pallas kernels, gather_pages(): pl.pallas_call(lambda *refs: gather_kernel(pool_rows, places, *refs), in_...  2.36 us
    ppermute x4, starting transfers between devices, swapped(): return lax.ppermute(shard, 'batch', [(c, c ^ bit) for c in range(count)])  2.23 us
    pallas_call x1, Pallas kernels, tables(): pl.pallas_call(lambda *refs: tables_kernel(rows, steps, segs, prefix_len,...  2.04 us
    ppermute x1, waiting for transfers between devices, per_device(): lax.ppermute(swapped_value[:, :split], 'blk', [(j, j + 2) for j in range(...  2.01 us
  transfers between devices with their start and end apart: 10, of which 3 were waited for; matrix products, arithmetic and copies ran while one was open for 4% of the time, Pallas kernels for 35%

commit v1 on v0

--- a/solution.py
+++ b/solution.py
@@ -562,7 +562,7 @@
     )
     to_swap = jnp.where(even, keys, far[0])
     far_key = lax.ppermute(to_swap, "blk", swap)
-    split = values.shape[1] * 3 // 4
+    split = values.shape[1] // 2
     passed_value = lax.ppermute(
         swapped_value[:, :split], "blk", [(j, j + 2) for j in range(0, blocks - 2, 2)]
     )

time: 41.1 us -> 44.6 us (1.085); the launches traced: 40.3 us -> 44.4 us
  waiting for transfers between devices: 3.26 us -> 6.4 us
  starting transfers between devices: 16.1 us -> 16.9 us
    ppermute x1, waiting for transfers between devices: 0.01 us -> 5.51 us  [per_device(): far_key = lax.ppermute(to_swap, 'blk', swap)]
    ppermute x1, waiting for transfers between devices: 2.01 us -> 0.01 us  [per_device(): lax.ppermute(swapped_value[:, :split], 'blk', [(j, j + 2) for j in range(...]
    ppermute x2, waiting for transfers between devices: 0.95 us -> 0.01 us  [shifted(): lax.ppermute(value, 'blk', [(source, source + steps) for source in range(...]
    ppermute x1, starting transfers between devices: 0.6 us -> 1.49 us  [per_device(): far_key = lax.ppermute(to_swap, 'blk', swap)]
    ppermute x1, waiting for transfers between devices: 0.28 us -> 0.87 us  [per_device(): swapped_value = lax.ppermute(values, 'blk', swap)]
  transfers between devices with their start and end apart: 10 -> 10, of which waited for: 3 -> 2; matrix products, arithmetic and copies ran while one was open for 4% -> 4% of each run, Pallas kernels for 35% -> 32%
where the time goes in v1:
time: 44.6 us; the launch traced here: 44.4 us
  Pallas kernels  18.5 us (41%)
  starting transfers between devices  16.9 us (38%)
  waiting for transfers between devices  6.4 us (14%)
  local copies, waits for them, and re-layouts  0.86 us (2%)
  between operations  0.83 us (2%)
  other arithmetic  0.82 us (2%)
    pallas_call x2, Pallas kernels, join(): pl.pallas_call(kernel, grid=(KEY_VALUE_HEADS // HEADS_PER_STEP,), in_spec...  9.49 us
    ppermute x2, starting transfers between devices, shifted(): lax.ppermute(value, 'blk', [(source, source + steps) for source in range(...  6.96 us
    ppermute x1, waiting for transfers between devices, per_device(): far_key = lax.ppermute(to_swap, 'blk', swap)  5.51 us
    ppermute x1, starting transfers between devices, per_device(): lax.ppermute(swapped_value[:, :split], 'blk', [(j, j + 2) for j in range(...  3.48 us
    pallas_call x1, Pallas kernels, attend_own(): pl.pallas_call(lambda *refs: own_kernel(rows, *refs), grid=(KEY_VALUE_HEA...  2.79 us
    pallas_call x1, Pallas kernels, gather_pages(): pl.pallas_call(lambda *refs: gather_kernel(pool_rows, places, *refs), in_...  2.36 us
    ppermute x4, starting transfers between devices, swapped(): return lax.ppermute(shard, 'batch', [(c, c ^ bit) for c in range(count)])  2.23 us
    pallas_call x1, Pallas kernels, tables(): pl.pallas_call(lambda *refs: tables_kernel(rows, steps, segs, prefix_len,...  2.04 us
  transfers between devices with their start and end apart: 10, of which 2 were waited for; matrix products, arithmetic and copies ran while one was open for 4% of the time, Pallas kernels for 32%

profile of v1, /device:TPU:8, one launch (start us, length us, event | category | flops | bytes accessed | tf_op | source)
XLA Modules:
  0.0 44.4 jit_solution(2409202943255060248)
XLA Ops:
  0.6 3.5 %collective-permute-start.2 = (bf16[1,256,1024]{2,1,0:T(8,128)(2,1)}, bf16[1,256,1024]{2,1,0:T(8,128)(2,1)S(1)}, u32[]{:S(2)}, u32[]{:S(2)}) collective-permute-start(bf16[1,256,1024]{2,1,0:T(8,128)(2,1)} %refs_3_.1), channel_id=1, source_target_pairs={{0,8},{4,12},{8,16},{12,20},{16,24},{20,28},{1,9},{5,13},{9,17},{1... | collective-permute-start | bytes 1572872 | tf_op jit(solution)/shard_map/ppermute | solution.py:45
  4.1 0.1 collective-permute-start
  4.2 1.6 %collective-permute-start.1 = (bf16[8,16,2048]{2,1,0:T(8,128)(2,1)}, bf16[8,16,2048]{2,1,0:T(8,128)(2,1)S(1)}, u32[]{:S(2)}, u32[]{:S(2)}) collective-permute-start(bf16[8,16,2048]{2,1,0:T(8,128)(2,1)} %refs_5_.1), channel_id=1, source_target_pairs={{0,2},{1,3},{2,0},{3,1},{4,6},{5,7},{6,4},{7,5},{8,10},{9,11},{10,... | collective-permute-start | bytes 1572872 | tf_op jit(solution)/shard_map/ppermute | solution.py:527
  5.8 1.5 %collective-permute-start.3 = (bf16[1,256,1024]{2,1,0:T(8,128)(2,1)}, bf16[1,256,1024]{2,1,0:T(8,128)(2,1)S(1)}, u32[]{:S(2)}, u32[]{:S(2)}) collective-permute-start(bf16[1,256,1024]{2,1,0:T(8,128)(2,1)} %refs_4_.1), channel_id=1, source_target_pairs={{0,4},{4,0},{8,12},{12,8},{16,20},{20,16},{24,28},{28,24},{1,5},{5... | collective-permute-start | bytes 1572872 | tf_op jit(solution)/shard_map/ppermute | solution.py:555
  7.3 3.5 %collective-permute-start.6 = (bf16[1,256,1024]{2,1,0:T(8,128)(2,1)}, bf16[1,256,1024]{2,1,0:T(8,128)(2,1)S(1)}, u32[]{:S(2)}, u32[]{:S(2)}) collective-permute-start(bf16[1,256,1024]{2,1,0:T(8,128)(2,1)} %refs_4_.1), channel_id=1, source_target_pairs={{0,8},{4,12},{8,16},{12,20},{16,24},{20,28},{1,9},{5,13},{9,17},{1... | collective-permute-start | bytes 1572872 | tf_op jit(solution)/shard_map/ppermute | solution.py:45
  10.8 0.8 %reshape.15 = s32[56]{0:T(128)S(1)} reshape(s32[4,2,7]{2,1,0:T(2,128)} %bitcast.3) | data formatting | bytes 448 | tf_op jit(solution)/shard_map/reshape | solution.py:556
  11.5 0.8 %pad_add_fusion.refs_0_ = s32[65]{0:T(128)S(1)} fusion(s32[56]{0:T(128)S(1)} %reshape.15, s32[2]{0:T(128)} %bitcast.4, s32[7]{0:T(128)} %bitcast.5), kind=kLoop, calls=%fused_computation.1 | loop fusion | flops 130 | bytes 520 | tf_op jit(solution)/shard_map/concatenate | solution.py:556
  12.3 0.0 copy-start
  12.3 0.0 copy-start.1
  12.3 0.0 copy-start.2
  12.3 0.0 copy-start.3
  12.3 2.0 %tables.1 = (s32[14]{0:T(128)S(1)}, f32[256,128]{1,0:T(8,128)S(1)}, f32[256,128]{1,0:T(8,128)S(1)}, f32[256,128]{1,0:T(8,128)S(1)}, f32[256,128]{1,0:T(8,128)S(1...) custom-call(s32[65]{0:T(128)S(1)} %pad_add_fusion.refs_0_), custom_call_target="tpu_custom_call" | custom-call | flops 2000000000 | tf_op jit(solution)/shard_map/tables/pallas_call | solution.py:159
  14.4 0.0 copy-done
  14.4 0.0 copy-done.1
  14.4 0.0 copy-done.2
  14.4 0.0 copy-done.3
  14.4 1.8 %prepare.1 = (bf16[1,256,2048]{2,1,0:T(8,128)(2,1)S(1)}, bf16[1,256,1024]{2,1,0:T(8,128)(2,1)}, bf16[1,256,1024]{2,1,0:T(8,128)(2,1)S(1)}, bf16[1,256,1024]{2,1,0:T(8,128)(2,1)S(1)}, bf16[8,16,2048]{2,1,0:T(8,128)(2,1)S(1)}) custom-call(f32[256,128]{1,0:T(8,128)S(1)} %get-tuple-element.35.refs_0_, f32[256,128]{1,0:T(8,128)S(1)} %get-tuple-element.36.refs_1_, ...), custom_call_target="tpu_custom_call" | custom-call | tf_op jit(solution)/shard_map/prepare/pallas_call | solution.py:199
  16.2 2.8 %own.1 = (f32[256,2048]{1,0:T(8,128)S(1)}, f32[256,128]{1,0:T(8,128)S(1)}) custom-call(f32[256,256]{1,0:T(8,128)S(1)} %get-tuple-element.34.refs_0_, bf16[1,256,2048]{2,1,0:T(8,128)(2,1)S(1)} %get-tuple-element.37.refs_1_.refs_5_, bf16[1,256,1024]{2,1,0:T(8,128)(2,1)S(1)} %get-tuple-element.38.refs_2_, bf16[1,256,1024]{2,1,0:T(8,128)(2,1)S(1)} %get-tuple-element.39.refs_3_), custom_call_target="tpu_custom_call" | custom-call | tf_op jit(solution)/shard_map/own/pallas_call | solution.py:302
  19.0 0.0 collective-permute-done.2.refs_8_
  19.0 0.1 broadcast_select_fusion
  19.1 0.0 collective-permute-done.refs_2_
  19.1 0.0 collective-permute-done.1.refs_3_
  19.1 0.9 %collective-permute-done.3.refs_7_ = bf16[1,256,1024]{2,1,0:T(8,128)(2,1)S(1)} collective-permute-done((bf16[1,256,1024]{2,1,0:T(8,128)(2,1)}, bf16[1,256,1024]{2,1,0:T(8,128)(2,1)S(1)}, u32[]{:S(2)}, u32[]{:S(2)}) %collective-permute-start.3) | collective-permute-done | bytes 524320 | tf_op jit(solution)/shard_map/ppermute | solution.py:555
  20.0 0.1 collective-permute-start.4
  20.1 0.5 %collective-permute-start.5 = (bf16[4,16,2048]{2,1,0:T(8,128)(2,1)S(1)}, bf16[4,16,2048]{2,1,0:T(8,128)(2,1)S(1)}, u32[]{:S(2)}, u32[]{:S(2)}) collective-permute-start(bf16[4,16,2048]{2,1,0:T(8,128)(2,1)S(1)} %get-tuple-element.54), channel_id=1, source_target_pairs={{0,1},{1,0},{2,3},{3,2},{4,5},{5,4},{6,7},{7,6},{8,9},{9,8},{10,11... | collective-permute-start | bytes 786440 | tf_op jit(solution)/shard_map/ppermute | solution.py:527
  20.6 1.5 %collective-permute-start.7 = (bf16[1,256,1024]{2,1,0:T(8,128)(2,1)S(1)}, bf16[1,256,1024]{2,1,0:T(8,128)(2,1)S(1)}, u32[]{:S(2)}, u32[]{:S(2)}) collective-permute-start(bf16[1,256,1024]{2,1,0:T(8,128)(2,1)S(1)} %broadcast_select_fusion), channel_id=1, source_target_pairs={{0,4},{4,0},{8,12},{12,8},{16,20},{20,16},{24,28},{28,24},{1,5},{5... | collective-permute-start | bytes 1572872 | tf_op jit(solution)/shard_map/ppermute | solution.py:564
  22.1 3.5 %collective-permute-start.8 = (bf16[1,128,1024]{2,1,0:T(8,128)(2,1)S(1)}, bf16[1,128,1024]{2,1,0:T(8,128)(2,1)S(1)}, u32[]{:S(2)}, u32[]{:S(2)}) collective-permute-start(bf16[1,128,1024]{2,1,0:T(8,128)(2,1)S(1)} %slice.16), channel_id=1, source_target_pairs={{0,8},{8,16},{16,24},{1,9},{9,17},{17,25},{2,10},{10,18},{18,26},{... | collective-permute-start | bytes 786440 | tf_op jit(solution)/shard_map/ppermute | solution.py:566
  25.6 0.0 collective-permute-done.4.refs_4_
  25.7 0.0 collective-permute-done.5.refs_5_
  25.7 1.3 %collective-permute-start.9 = (bf16[1,128,1024]{2,1,0:T(8,128)(2,1)S(1)}, bf16[1,128,1024]{2,1,0:T(8,128)(2,1)S(1)}, u32[]{:S(2)}, u32[]{:S(2)}) collective-permute-start(bf16[1,128,1024]{2,1,0:T(8,128)(2,1)S(1)} %slice.14), channel_id=1, source_target_pairs={{4,8},{12,16},{20,24},{5,9},{13,17},{21,25},{6,10},{14,18},{22,26}... | collective-permute-start | bytes 786440 | tf_op jit(solution)/shard_map/ppermute | solution.py:575
  27.0 2.4 %gather.1.refs_6_.refs_7_ = bf16[14,16,2048]{2,1,0:T(8,128)(2,1)S(1)} custom-call(s32[14]{0:T(128)S(1)} %get-tuple-element.42.refs_0_, bf16[8,16,2048]{2,1,0:T(8,128)(2,1)S(1)} %get-tuple-element.43.refs_1_, bf16[8,16,2048]{2,1,0:T(8,128)(2,1)S(1)} %collective-permute-done.refs_2_, bf16[8,16,2048]{2,1,0:T(8,128)(2,1)S(1)} %collective-permute-done.1.refs_3_, ...), custom_call_target="tpu_custom_call" | custom-call | tf_op jit(solution)/shard_map/gather/pallas_call | solution.py:351
  29.3 0.0 collective-permute-done.6.refs_9_
  29.3 5.3 %far.1 = (f32[256,2048]{1,0:T(8,128)S(1)}, f32[256,128]{1,0:T(8,128)S(1)}) custom-call(f32[256,128]{1,0:T(8,128)S(1)} %get-tuple-element.31.refs_0_, f32[256,128]{1,0:T(8,128)S(1)} %get-tuple-element.32.refs_1_, f32[256,512]{1,0:T(8,128)S(1)} %get-tuple-element.33.refs_2_, f32[256,128]{1,0:T(8,128)S(1)} %get-tuple-element.40.refs_3_, ...), custom_call_target="tpu_custom_call" | custom-call | tf_op jit(solution)/shard_map/far/pallas_call | solution.py:510
  34.6 0.0 collective-permute-done.8.refs_8_
  34.6 5.5 %collective-permute-done.7.refs_6_ = bf16[1,256,1024]{2,1,0:T(8,128)(2,1)S(1)} collective-permute-done((bf16[1,256,1024]{2,1,0:T(8,128)(2,1)S(1)}, bf16[1,256,1024]{2,1,0:T(8,128)(2,1)S(1)}, u32[]{:S(2)}, u32[]{:S(2)}) %collective-permute-start.7) | collective-permute-done | bytes 524320 | tf_op jit(solution)/shard_map/ppermute | solution.py:564
  40.1 0.0 collective-permute-done.9.refs_9_
  40.1 4.2 %last.1 = bf16[1,256,2048]{2,1,0:T(8,128)(2,1)} custom-call(f32[256,128]{1,0:T(8,128)S(1)} %get-tuple-element.28.refs_0_, f32[256,128]{1,0:T(8,128)S(1)} %get-tuple-element.29.refs_1_, f32[256,256]{1,0:T(8,128)S(1)} %get-tuple-element.30.refs_2_, f32[256,128]{1,0:T(8,128)S(1)} %get-tuple-element.50.refs_3_, f32[256,2048]{1,0:T(8,128)S(1)} %get-tuple-element.51.refs_4_, ...), custom_call_target="tpu_custom_call" | custom-call | tf_op jit(solution)/shard_map/last/pallas_call | solution.py:510
  (3 shorter events, 0.1 us)
Async XLA Ops:
  0.6 18.4 %collective-permute-start.2 = (bf16[1,256,1024]{2,1,0:T(8,128)(2,1)}, bf16[1,256,1024]{2,1,0:T(8,128)(2,1)S(1)}, u32[]{:S(2)}, u32[]{:S(2)}) collective-permute-start(bf16[1,256,1024]{2,1,0:T(8,128)(2,1)} %refs_3_.1), channel_id=1, source_target_pairs={{0,8},{4,12},{8,16},{12,20},{16,24},{20,28},{1,9},{5,13},{9,17},{1... | collective-permute-start | bytes 1572872 | tf_op jit(solution)/shard_map/ppermute | solution.py:45
  4.1 15.0 %collective-permute-start = (bf16[8,16,2048]{2,1,0:T(8,128)(2,1)}, bf16[8,16,2048]{2,1,0:T(8,128)(2,1)S(1)}, u32[]{:S(2)}, u32[]{:S(2)}) collective-permute-start(bf16[8,16,2048]{2,1,0:T(8,128)(2,1)} %refs_5_.1), channel_id=1, source_target_pairs={{0,1},{1,0},{2,3},{3,2},{4,5},{5,4},{6,7},{7,6},{8,9},{9,8},{10,11... | collective-permute-start | bytes 1572872 | tf_op jit(solution)/shard_map/ppermute | solution.py:527
  4.2 14.9 %collective-permute-start.1 = (bf16[8,16,2048]{2,1,0:T(8,128)(2,1)}, bf16[8,16,2048]{2,1,0:T(8,128)(2,1)S(1)}, u32[]{:S(2)}, u32[]{:S(2)}) collective-permute-start(bf16[8,16,2048]{2,1,0:T(8,128)(2,1)} %refs_5_.1), channel_id=1, source_target_pairs={{0,2},{1,3},{2,0},{3,1},{4,6},{5,7},{6,4},{7,5},{8,10},{9,11},{10,... | collective-permute-start | bytes 1572872 | tf_op jit(solution)/shard_map/ppermute | solution.py:527
  5.8 14.2 %collective-permute-start.3 = (bf16[1,256,1024]{2,1,0:T(8,128)(2,1)}, bf16[1,256,1024]{2,1,0:T(8,128)(2,1)S(1)}, u32[]{:S(2)}, u32[]{:S(2)}) collective-permute-start(bf16[1,256,1024]{2,1,0:T(8,128)(2,1)} %refs_4_.1), channel_id=1, source_target_pairs={{0,4},{4,0},{8,12},{12,8},{16,20},{20,16},{24,28},{28,24},{1,5},{5... | collective-permute-start | bytes 1572872 | tf_op jit(solution)/shard_map/ppermute | solution.py:555
  7.3 22.0 %collective-permute-start.6 = (bf16[1,256,1024]{2,1,0:T(8,128)(2,1)}, bf16[1,256,1024]{2,1,0:T(8,128)(2,1)S(1)}, u32[]{:S(2)}, u32[]{:S(2)}) collective-permute-start(bf16[1,256,1024]{2,1,0:T(8,128)(2,1)} %refs_4_.1), channel_id=1, source_target_pairs={{0,8},{4,12},{8,16},{12,20},{16,24},{20,28},{1,9},{5,13},{9,17},{1... | collective-permute-start | bytes 1572872 | tf_op jit(solution)/shard_map/ppermute | solution.py:45
  12.3 2.1 %copy-start = (bf16[1,256,1024]{2,1,0:T(8,128)(2,1)S(1)}, bf16[1,256,1024]{2,1,0:T(8,128)(2,1)}, u32[]{:S(2)}) copy-start(bf16[1,256,1024]{2,1,0:T(8,128)(2,1)} %refs_3_.1) | copy-start | bytes 1572868
  12.3 2.1 %copy-start.1 = (bf16[1,256,1024]{2,1,0:T(8,128)(2,1)S(1)}, bf16[1,256,1024]{2,1,0:T(8,128)(2,1)}, u32[]{:S(2)}) copy-start(bf16[1,256,1024]{2,1,0:T(8,128)(2,1)} %refs_4_.1) | copy-start | bytes 1572868
  12.3 2.1 %copy-start.2 = (bf16[1,256,2048]{2,1,0:T(8,128)(2,1)S(1)}, bf16[1,256,2048]{2,1,0:T(8,128)(2,1)}, u32[]{:S(2)}) copy-start(bf16[1,256,2048]{2,1,0:T(8,128)(2,1)} %refs_2_.1) | copy-start | bytes 3145732
  12.3 2.1 %copy-start.3 = (bf16[8,16,2048]{2,1,0:T(8,128)(2,1)S(1)}, bf16[8,16,2048]{2,1,0:T(8,128)(2,1)}, u32[]{:S(2)}) copy-start(bf16[8,16,2048]{2,1,0:T(8,128)(2,1)} %refs_5_.1) | copy-start | bytes 1572868
  20.0 5.6 %collective-permute-start.4 = (bf16[4,16,2048]{2,1,0:T(8,128)(2,1)S(1)}, bf16[4,16,2048]{2,1,0:T(8,128)(2,1)S(1)}, u32[]{:S(2)}, u32[]{:S(2)}) collective-permute-start(bf16[4,16,2048]{2,1,0:T(8,128)(2,1)S(1)} %get-tuple-element.55), channel_id=1, source_target_pairs={{0,1},{1,0},{2,3},{3,2},{4,5},{5,4},{6,7},{7,6},{8,9},{9,8},{10,11... | collective-permute-start | bytes 786440 | tf_op jit(solution)/shard_map/ppermute | solution.py:527
  20.1 5.5 %collective-permute-start.5 = (bf16[4,16,2048]{2,1,0:T(8,128)(2,1)S(1)}, bf16[4,16,2048]{2,1,0:T(8,128)(2,1)S(1)}, u32[]{:S(2)}, u32[]{:S(2)}) collective-permute-start(bf16[4,16,2048]{2,1,0:T(8,128)(2,1)S(1)} %get-tuple-element.54), channel_id=1, source_target_pairs={{0,1},{1,0},{2,3},{3,2},{4,5},{5,4},{6,7},{7,6},{8,9},{9,8},{10,11... | collective-permute-start | bytes 786440 | tf_op jit(solution)/shard_map/ppermute | solution.py:527
  20.6 19.5 %collective-permute-start.7 = (bf16[1,256,1024]{2,1,0:T(8,128)(2,1)S(1)}, bf16[1,256,1024]{2,1,0:T(8,128)(2,1)S(1)}, u32[]{:S(2)}, u32[]{:S(2)}) collective-permute-start(bf16[1,256,1024]{2,1,0:T(8,128)(2,1)S(1)} %broadcast_select_fusion), channel_id=1, source_target_pairs={{0,4},{4,0},{8,12},{12,8},{16,20},{20,16},{24,28},{28,24},{1,5},{5... | collective-permute-start | bytes 1572872 | tf_op jit(solution)/shard_map/ppermute | solution.py:564
  22.1 12.5 %collective-permute-start.8 = (bf16[1,128,1024]{2,1,0:T(8,128)(2,1)S(1)}, bf16[1,128,1024]{2,1,0:T(8,128)(2,1)S(1)}, u32[]{:S(2)}, u32[]{:S(2)}) collective-permute-start(bf16[1,128,1024]{2,1,0:T(8,128)(2,1)S(1)} %slice.16), channel_id=1, source_target_pairs={{0,8},{8,16},{16,24},{1,9},{9,17},{17,25},{2,10},{10,18},{18,26},{... | collective-permute-start | bytes 786440 | tf_op jit(solution)/shard_map/ppermute | solution.py:566
  25.7 14.5 %collective-permute-start.9 = (bf16[1,128,1024]{2,1,0:T(8,128)(2,1)S(1)}, bf16[1,128,1024]{2,1,0:T(8,128)(2,1)S(1)}, u32[]{:S(2)}, u32[]{:S(2)}) collective-permute-start(bf16[1,128,1024]{2,1,0:T(8,128)(2,1)S(1)} %slice.14), channel_id=1, source_target_pairs={{4,8},{12,16},{20,24},{5,9},{13,17},{21,25},{6,10},{14,18},{22,26}... | collective-permute-start | bytes 786440 | tf_op jit(solution)/shard_map/ppermute | solution.py:575

commit v2 on v1

--- a/solution.py
+++ b/solution.py
@@ -562,7 +562,7 @@
     )
     to_swap = jnp.where(even, keys, far[0])
     far_key = lax.ppermute(to_swap, "blk", swap)
-    split = values.shape[1] // 2
+    split = values.shape[1] * 9 // 16
     passed_value = lax.ppermute(
         swapped_value[:, :split], "blk", [(j, j + 2) for j in range(0, blocks - 2, 2)]
     )

time: 44.6 us -> 42 us (0.942)
  waiting for transfers between devices: 6.4 us -> 4.71 us
  starting transfers between devices: 16.9 us -> 16.1 us
    ppermute x1, waiting for transfers between devices: 5.51 us -> 3.14 us  [per_device(): far_key = lax.ppermute(to_swap, 'blk', swap)]
    ppermute x2, waiting for transfers between devices: 0.01 us -> 0.95 us  [shifted(): lax.ppermute(value, 'blk', [(source, source + steps) for source in range(...]
    ppermute x1, starting transfers between devices: 1.49 us -> 0.6 us  [per_device(): far_key = lax.ppermute(to_swap, 'blk', swap)]
    ppermute x1, waiting for transfers between devices: 0.87 us -> 0.28 us  [per_device(): swapped_value = lax.ppermute(values, 'blk', swap)]
  transfers between devices with their start and end apart: 10 -> 10, of which waited for: 2 -> 4; matrix products, arithmetic and copies ran while one was open for 4% -> 4% of each run, Pallas kernels for 32% -> 34%
where the time goes in v2:
time: 42 us; the launch traced here: 41.7 us
  Pallas kernels  18.5 us (44%)
  starting transfers between devices  16.1 us (38%)
  waiting for transfers between devices  4.71 us (11%)
  local copies, waits for them, and re-layouts  0.86 us (2%)
  other arithmetic  0.82 us (2%)
  between operations  0.81 us (2%)
    pallas_call x2, Pallas kernels, join(): pl.pallas_call(kernel, grid=(KEY_VALUE_HEADS // HEADS_PER_STEP,), in_spec...  9.47 us
    ppermute x2, starting transfers between devices, shifted(): lax.ppermute(value, 'blk', [(source, source + steps) for source in range(...  6.96 us
    ppermute x1, starting transfers between devices, per_device(): lax.ppermute(swapped_value[:, :split], 'blk', [(j, j + 2) for j in range(...  3.48 us
    ppermute x1, waiting for transfers between devices, per_device(): far_key = lax.ppermute(to_swap, 'blk', swap)  3.14 us
    pallas_call x1, Pallas kernels, attend_own(): pl.pallas_call(lambda *refs: own_kernel(rows, *refs), grid=(KEY_VALUE_HEA...  2.79 us
    pallas_call x1, Pallas kernels, gather_pages(): pl.pallas_call(lambda *refs: gather_kernel(pool_rows, places, *refs), in_...  2.36 us
    ppermute x4, starting transfers between devices, swapped(): return lax.ppermute(shard, 'batch', [(c, c ^ bit) for c in range(count)])  2.23 us
    pallas_call x1, Pallas kernels, tables(): pl.pallas_call(lambda *refs: tables_kernel(rows, steps, segs, prefix_len,...  2.04 us
  transfers between devices with their start and end apart: 10, of which 4 were waited for; matrix products, arithmetic and copies ran while one was open for 4% of the time, Pallas kernels for 34%

profile of v2, /device:TPU:8, one launch (start us, length us, event | category | flops | bytes accessed | tf_op | source)
XLA Modules:
  0.0 41.7 jit_solution(12236782254710838003)
XLA Ops:
  0.6 3.5 %collective-permute-start.2 = (bf16[1,256,1024]{2,1,0:T(8,128)(2,1)}, bf16[1,256,1024]{2,1,0:T(8,128)(2,1)S(1)}, u32[]{:S(2)}, u32[]{:S(2)}) collective-permute-start(bf16[1,256,1024]{2,1,0:T(8,128)(2,1)} %refs_3_.1), channel_id=1, source_target_pairs={{0,8},{4,12},{8,16},{12,20},{16,24},{20,28},{1,9},{5,13},{9,17},{1... | collective-permute-start | bytes 1572872 | tf_op jit(solution)/shard_map/ppermute | solution.py:45
  4.1 0.1 collective-permute-start
  4.2 1.6 %collective-permute-start.1 = (bf16[8,16,2048]{2,1,0:T(8,128)(2,1)}, bf16[8,16,2048]{2,1,0:T(8,128)(2,1)S(1)}, u32[]{:S(2)}, u32[]{:S(2)}) collective-permute-start(bf16[8,16,2048]{2,1,0:T(8,128)(2,1)} %refs_5_.1), channel_id=1, source_target_pairs={{0,2},{1,3},{2,0},{3,1},{4,6},{5,7},{6,4},{7,5},{8,10},{9,11},{10,... | collective-permute-start | bytes 1572872 | tf_op jit(solution)/shard_map/ppermute | solution.py:527
  5.8 1.5 %collective-permute-start.3 = (bf16[1,256,1024]{2,1,0:T(8,128)(2,1)}, bf16[1,256,1024]{2,1,0:T(8,128)(2,1)S(1)}, u32[]{:S(2)}, u32[]{:S(2)}) collective-permute-start(bf16[1,256,1024]{2,1,0:T(8,128)(2,1)} %refs_4_.1), channel_id=1, source_target_pairs={{0,4},{4,0},{8,12},{12,8},{16,20},{20,16},{24,28},{28,24},{1,5},{5... | collective-permute-start | bytes 1572872 | tf_op jit(solution)/shard_map/ppermute | solution.py:555
  7.3 3.5 %collective-permute-start.6 = (bf16[1,256,1024]{2,1,0:T(8,128)(2,1)}, bf16[1,256,1024]{2,1,0:T(8,128)(2,1)S(1)}, u32[]{:S(2)}, u32[]{:S(2)}) collective-permute-start(bf16[1,256,1024]{2,1,0:T(8,128)(2,1)} %refs_4_.1), channel_id=1, source_target_pairs={{0,8},{4,12},{8,16},{12,20},{16,24},{20,28},{1,9},{5,13},{9,17},{1... | collective-permute-start | bytes 1572872 | tf_op jit(solution)/shard_map/ppermute | solution.py:45
  10.8 0.8 %reshape.15 = s32[56]{0:T(128)S(1)} reshape(s32[4,2,7]{2,1,0:T(2,128)} %bitcast.3) | data formatting | bytes 448 | tf_op jit(solution)/shard_map/reshape | solution.py:556
  11.5 0.8 %pad_add_fusion.refs_0_ = s32[65]{0:T(128)S(1)} fusion(s32[56]{0:T(128)S(1)} %reshape.15, s32[2]{0:T(128)} %bitcast.4, s32[7]{0:T(128)} %bitcast.5), kind=kLoop, calls=%fused_computation.1 | loop fusion | flops 130 | bytes 520 | tf_op jit(solution)/shard_map/concatenate | solution.py:556
  12.3 0.0 copy-start
  12.3 0.0 copy-start.1
  12.3 0.0 copy-start.2
  12.3 0.0 copy-start.3
  12.3 2.0 %tables.1 = (s32[14]{0:T(128)S(1)}, f32[256,128]{1,0:T(8,128)S(1)}, f32[256,128]{1,0:T(8,128)S(1)}, f32[256,128]{1,0:T(8,128)S(1)}, f32[256,128]{1,0:T(8,128)S(1...) custom-call(s32[65]{0:T(128)S(1)} %pad_add_fusion.refs_0_), custom_call_target="tpu_custom_call" | custom-call | flops 2000000000 | tf_op jit(solution)/shard_map/tables/pallas_call | solution.py:159
  14.4 0.0 copy-done
  14.4 0.0 copy-done.1
  14.4 0.0 copy-done.2
  14.4 0.0 copy-done.3
  14.4 1.8 %prepare.1 = (bf16[1,256,2048]{2,1,0:T(8,128)(2,1)S(1)}, bf16[1,256,1024]{2,1,0:T(8,128)(2,1)}, bf16[1,256,1024]{2,1,0:T(8,128)(2,1)S(1)}, bf16[1,256,1024]{2,1,0:T(8,128)(2,1)S(1)}, bf16[8,16,2048]{2,1,0:T(8,128)(2,1)S(1)}) custom-call(f32[256,128]{1,0:T(8,128)S(1)} %get-tuple-element.35.refs_0_, f32[256,128]{1,0:T(8,128)S(1)} %get-tuple-element.36.refs_1_, ...), custom_call_target="tpu_custom_call" | custom-call | tf_op jit(solution)/shard_map/prepare/pallas_call | solution.py:199
  16.2 2.8 %own.1 = (f32[256,2048]{1,0:T(8,128)S(1)}, f32[256,128]{1,0:T(8,128)S(1)}) custom-call(f32[256,256]{1,0:T(8,128)S(1)} %get-tuple-element.34.refs_0_, bf16[1,256,2048]{2,1,0:T(8,128)(2,1)S(1)} %get-tuple-element.37.refs_1_.refs_5_, bf16[1,256,1024]{2,1,0:T(8,128)(2,1)S(1)} %get-tuple-element.38.refs_2_, bf16[1,256,1024]{2,1,0:T(8,128)(2,1)S(1)} %get-tuple-element.39.refs_3_), custom_call_target="tpu_custom_call" | custom-call | tf_op jit(solution)/shard_map/own/pallas_call | solution.py:302
  19.0 0.0 collective-permute-done.2.refs_8_
  19.0 0.1 broadcast_select_fusion
  19.1 0.6 %collective-permute-start.7 = (bf16[1,256,1024]{2,1,0:T(8,128)(2,1)S(1)}, bf16[1,256,1024]{2,1,0:T(8,128)(2,1)S(1)}, u32[]{:S(2)}, u32[]{:S(2)}) collective-permute-start(bf16[1,256,1024]{2,1,0:T(8,128)(2,1)S(1)} %broadcast_select_fusion), channel_id=1, source_target_pairs={{0,4},{4,0},{8,12},{12,8},{16,20},{20,16},{24,28},{28,24},{1,5},{5... | collective-permute-start | bytes 1572872 | tf_op jit(solution)/shard_map/ppermute | solution.py:564
  19.7 0.0 collective-permute-done.refs_2_
  19.7 0.0 collective-permute-done.1.refs_3_
  19.7 0.3 collective-permute-done.3.refs_7_
  20.0 0.1 collective-permute-start.4
  20.1 0.5 %collective-permute-start.5 = (bf16[4,16,2048]{2,1,0:T(8,128)(2,1)S(1)}, bf16[4,16,2048]{2,1,0:T(8,128)(2,1)S(1)}, u32[]{:S(2)}, u32[]{:S(2)}) collective-permute-start(bf16[4,16,2048]{2,1,0:T(8,128)(2,1)S(1)} %get-tuple-element.54), channel_id=1, source_target_pairs={{0,1},{1,0},{2,3},{3,2},{4,5},{5,4},{6,7},{7,6},{8,9},{9,8},{10,11... | collective-permute-start | bytes 786440 | tf_op jit(solution)/shard_map/ppermute | solution.py:527
  20.6 3.5 %collective-permute-start.8 = (bf16[1,144,1024]{2,1,0:T(8,128)(2,1)S(1)}, bf16[1,144,1024]{2,1,0:T(8,128)(2,1)S(1)}, u32[]{:S(2)}, u32[]{:S(2)}) collective-permute-start(bf16[1,144,1024]{2,1,0:T(8,128)(2,1)S(1)} %slice.16), channel_id=1, source_target_pairs={{0,8},{8,16},{16,24},{1,9},{9,17},{17,25},{2,10},{10,18},{18,26},{... | collective-permute-start | bytes 884744 | tf_op jit(solution)/shard_map/ppermute | solution.py:566
  24.1 0.0 collective-permute-done.4.refs_4_
  24.2 0.0 collective-permute-done.5.refs_5_
  24.2 1.3 %collective-permute-start.9 = (bf16[1,112,1024]{2,1,0:T(8,128)(2,1)S(1)}, bf16[1,112,1024]{2,1,0:T(8,128)(2,1)S(1)}, u32[]{:S(2)}, u32[]{:S(2)}) collective-permute-start(bf16[1,112,1024]{2,1,0:T(8,128)(2,1)S(1)} %slice.14), channel_id=1, source_target_pairs={{4,8},{12,16},{20,24},{5,9},{13,17},{21,25},{6,10},{14,18},{22,26}... | collective-permute-start | bytes 688136 | tf_op jit(solution)/shard_map/ppermute | solution.py:575
  25.5 2.4 %gather.1.refs_6_.refs_7_ = bf16[14,16,2048]{2,1,0:T(8,128)(2,1)S(1)} custom-call(s32[14]{0:T(128)S(1)} %get-tuple-element.42.refs_0_, bf16[8,16,2048]{2,1,0:T(8,128)(2,1)S(1)} %get-tuple-element.43.refs_1_, bf16[8,16,2048]{2,1,0:T(8,128)(2,1)S(1)} %collective-permute-done.refs_2_, bf16[8,16,2048]{2,1,0:T(8,128)(2,1)S(1)} %collective-permute-done.1.refs_3_, ...), custom_call_target="tpu_custom_call" | custom-call | tf_op jit(solution)/shard_map/gather/pallas_call | solution.py:351
  27.8 0.9 %collective-permute-done.6.refs_9_ = bf16[1,256,1024]{2,1,0:T(8,128)(2,1)S(1)} collective-permute-done((bf16[1,256,1024]{2,1,0:T(8,128)(2,1)}, bf16[1,256,1024]{2,1,0:T(8,128)(2,1)S(1)}, u32[]{:S(2)}, u32[]{:S(2)}) %collective-permute-start.6) | collective-permute-done | bytes 524320 | tf_op jit(solution)/shard_map/ppermute | solution.py:45
  28.8 5.2 %far.1 = (f32[256,2048]{1,0:T(8,128)S(1)}, f32[256,128]{1,0:T(8,128)S(1)}) custom-call(f32[256,128]{1,0:T(8,128)S(1)} %get-tuple-element.31.refs_0_, f32[256,128]{1,0:T(8,128)S(1)} %get-tuple-element.32.refs_1_, f32[256,512]{1,0:T(8,128)S(1)} %get-tuple-element.33.refs_2_, f32[256,128]{1,0:T(8,128)S(1)} %get-tuple-element.40.refs_3_, ...), custom_call_target="tpu_custom_call" | custom-call | tf_op jit(solution)/shard_map/far/pallas_call | solution.py:510
  34.0 0.0 collective-permute-done.8.refs_8_
  34.0 0.3 collective-permute-done.9.refs_9_
  34.4 3.1 %collective-permute-done.7.refs_6_ = bf16[1,256,1024]{2,1,0:T(8,128)(2,1)S(1)} collective-permute-done((bf16[1,256,1024]{2,1,0:T(8,128)(2,1)S(1)}, bf16[1,256,1024]{2,1,0:T(8,128)(2,1)S(1)}, u32[]{:S(2)}, u32[]{:S(2)}) %collective-permute-start.7) | collective-permute-done | bytes 524320 | tf_op jit(solution)/shard_map/ppermute | solution.py:564
  37.5 4.2 %last.1 = bf16[1,256,2048]{2,1,0:T(8,128)(2,1)} custom-call(f32[256,128]{1,0:T(8,128)S(1)} %get-tuple-element.28.refs_0_, f32[256,128]{1,0:T(8,128)S(1)} %get-tuple-element.29.refs_1_, f32[256,256]{1,0:T(8,128)S(1)} %get-tuple-element.30.refs_2_, f32[256,128]{1,0:T(8,128)S(1)} %get-tuple-element.50.refs_3_, f32[256,2048]{1,0:T(8,128)S(1)} %get-tuple-element.51.refs_4_, ...), custom_call_target="tpu_custom_call" | custom-call | tf_op jit(solution)/shard_map/last/pallas_call | solution.py:510
  (3 shorter events, 0.1 us)
Async XLA Ops:
  0.6 18.4 %collective-permute-start.2 = (bf16[1,256,1024]{2,1,0:T(8,128)(2,1)}, bf16[1,256,1024]{2,1,0:T(8,128)(2,1)S(1)}, u32[]{:S(2)}, u32[]{:S(2)}) collective-permute-start(bf16[1,256,1024]{2,1,0:T(8,128)(2,1)} %refs_3_.1), channel_id=1, source_target_pairs={{0,8},{4,12},{8,16},{12,20},{16,24},{20,28},{1,9},{5,13},{9,17},{1... | collective-permute-start | bytes 1572872 | tf_op jit(solution)/shard_map/ppermute | solution.py:45
  4.1 15.6 %collective-permute-start = (bf16[8,16,2048]{2,1,0:T(8,128)(2,1)}, bf16[8,16,2048]{2,1,0:T(8,128)(2,1)S(1)}, u32[]{:S(2)}, u32[]{:S(2)}) collective-permute-start(bf16[8,16,2048]{2,1,0:T(8,128)(2,1)} %refs_5_.1), channel_id=1, source_target_pairs={{0,1},{1,0},{2,3},{3,2},{4,5},{5,4},{6,7},{7,6},{8,9},{9,8},{10,11... | collective-permute-start | bytes 1572872 | tf_op jit(solution)/shard_map/ppermute | solution.py:527
  4.2 15.5 %collective-permute-start.1 = (bf16[8,16,2048]{2,1,0:T(8,128)(2,1)}, bf16[8,16,2048]{2,1,0:T(8,128)(2,1)S(1)}, u32[]{:S(2)}, u32[]{:S(2)}) collective-permute-start(bf16[8,16,2048]{2,1,0:T(8,128)(2,1)} %refs_5_.1), channel_id=1, source_target_pairs={{0,2},{1,3},{2,0},{3,1},{4,6},{5,7},{6,4},{7,5},{8,10},{9,11},{10,... | collective-permute-start | bytes 1572872 | tf_op jit(solution)/shard_map/ppermute | solution.py:527
  5.8 14.2 %collective-permute-start.3 = (bf16[1,256,1024]{2,1,0:T(8,128)(2,1)}, bf16[1,256,1024]{2,1,0:T(8,128)(2,1)S(1)}, u32[]{:S(2)}, u32[]{:S(2)}) collective-permute-start(bf16[1,256,1024]{2,1,0:T(8,128)(2,1)} %refs_4_.1), channel_id=1, source_target_pairs={{0,4},{4,0},{8,12},{12,8},{16,20},{20,16},{24,28},{28,24},{1,5},{5... | collective-permute-start | bytes 1572872 | tf_op jit(solution)/shard_map/ppermute | solution.py:555
  7.3 21.5 %collective-permute-start.6 = (bf16[1,256,1024]{2,1,0:T(8,128)(2,1)}, bf16[1,256,1024]{2,1,0:T(8,128)(2,1)S(1)}, u32[]{:S(2)}, u32[]{:S(2)}) collective-permute-start(bf16[1,256,1024]{2,1,0:T(8,128)(2,1)} %refs_4_.1), channel_id=1, source_target_pairs={{0,8},{4,12},{8,16},{12,20},{16,24},{20,28},{1,9},{5,13},{9,17},{1... | collective-permute-start | bytes 1572872 | tf_op jit(solution)/shard_map/ppermute | solution.py:45
  12.3 2.1 %copy-start = (bf16[1,256,1024]{2,1,0:T(8,128)(2,1)S(1)}, bf16[1,256,1024]{2,1,0:T(8,128)(2,1)}, u32[]{:S(2)}) copy-start(bf16[1,256,1024]{2,1,0:T(8,128)(2,1)} %refs_3_.1) | copy-start | bytes 1572868
  12.3 2.1 %copy-start.1 = (bf16[1,256,1024]{2,1,0:T(8,128)(2,1)S(1)}, bf16[1,256,1024]{2,1,0:T(8,128)(2,1)}, u32[]{:S(2)}) copy-start(bf16[1,256,1024]{2,1,0:T(8,128)(2,1)} %refs_4_.1) | copy-start | bytes 1572868
  12.3 2.1 %copy-start.2 = (bf16[1,256,2048]{2,1,0:T(8,128)(2,1)S(1)}, bf16[1,256,2048]{2,1,0:T(8,128)(2,1)}, u32[]{:S(2)}) copy-start(bf16[1,256,2048]{2,1,0:T(8,128)(2,1)} %refs_2_.1) | copy-start | bytes 3145732
  12.3 2.1 %copy-start.3 = (bf16[8,16,2048]{2,1,0:T(8,128)(2,1)S(1)}, bf16[8,16,2048]{2,1,0:T(8,128)(2,1)}, u32[]{:S(2)}) copy-start(bf16[8,16,2048]{2,1,0:T(8,128)(2,1)} %refs_5_.1) | copy-start | bytes 1572868
  19.1 18.4 %collective-permute-start.7 = (bf16[1,256,1024]{2,1,0:T(8,128)(2,1)S(1)}, bf16[1,256,1024]{2,1,0:T(8,128)(2,1)S(1)}, u32[]{:S(2)}, u32[]{:S(2)}) collective-permute-start(bf16[1,256,1024]{2,1,0:T(8,128)(2,1)S(1)} %broadcast_select_fusion), channel_id=1, source_target_pairs={{0,4},{4,0},{8,12},{12,8},{16,20},{20,16},{24,28},{28,24},{1,5},{5... | collective-permute-start | bytes 1572872 | tf_op jit(solution)/shard_map/ppermute | solution.py:564
  20.0 4.1 %collective-permute-start.4 = (bf16[4,16,2048]{2,1,0:T(8,128)(2,1)S(1)}, bf16[4,16,2048]{2,1,0:T(8,128)(2,1)S(1)}, u32[]{:S(2)}, u32[]{:S(2)}) collective-permute-start(bf16[4,16,2048]{2,1,0:T(8,128)(2,1)S(1)} %get-tuple-element.55), channel_id=1, source_target_pairs={{0,1},{1,0},{2,3},{3,2},{4,5},{5,4},{6,7},{7,6},{8,9},{9,8},{10,11... | collective-permute-start | bytes 786440 | tf_op jit(solution)/shard_map/ppermute | solution.py:527
  20.1 4.1 %collective-permute-start.5 = (bf16[4,16,2048]{2,1,0:T(8,128)(2,1)S(1)}, bf16[4,16,2048]{2,1,0:T(8,128)(2,1)S(1)}, u32[]{:S(2)}, u32[]{:S(2)}) collective-permute-start(bf16[4,16,2048]{2,1,0:T(8,128)(2,1)S(1)} %get-tuple-element.54), channel_id=1, source_target_pairs={{0,1},{1,0},{2,3},{3,2},{4,5},{5,4},{6,7},{7,6},{8,9},{9,8},{10,11... | collective-permute-start | bytes 786440 | tf_op jit(solution)/shard_map/ppermute | solution.py:527
  20.6 13.4 %collective-permute-start.8 = (bf16[1,144,1024]{2,1,0:T(8,128)(2,1)S(1)}, bf16[1,144,1024]{2,1,0:T(8,128)(2,1)S(1)}, u32[]{:S(2)}, u32[]{:S(2)}) collective-permute-start(bf16[1,144,1024]{2,1,0:T(8,128)(2,1)S(1)} %slice.16), channel_id=1, source_target_pairs={{0,8},{8,16},{16,24},{1,9},{9,17},{17,25},{2,10},{10,18},{18,26},{... | collective-permute-start | bytes 884744 | tf_op jit(solution)/shard_map/ppermute | solution.py:566
  24.2 10.2 %collective-permute-start.9 = (bf16[1,112,1024]{2,1,0:T(8,128)(2,1)S(1)}, bf16[1,112,1024]{2,1,0:T(8,128)(2,1)S(1)}, u32[]{:S(2)}, u32[]{:S(2)}) collective-permute-start(bf16[1,112,1024]{2,1,0:T(8,128)(2,1)S(1)} %slice.14), channel_id=1, source_target_pairs={{4,8},{12,16},{20,24},{5,9},{13,17},{21,25},{6,10},{14,18},{22,26}... | collective-permute-start | bytes 688136 | tf_op jit(solution)/shard_map/ppermute | solution.py:575

commit v3 on v0

--- a/solution.py
+++ b/solution.py
@@ -449,31 +449,63 @@
 
 def last_kernel(
     rows, cos_ref, sin_ref, bias_ref, level_ref, mean_ref, q_ref, key_ref, swapped_value,
-    passed_value, direct_value, out_ref, *refs,
+    passed_value, direct_value, out_ref, held, sem, *refs,
 ):
     work = split_work(refs)
     k_parts, v_parts = work[:2]
-    group = pl.program_id(0)
     even = lax.rem(lax.axis_index("blk"), 2) == 0
-
-    @pl.when(group == 0)
-    def _():
-        fill_ones(v_parts)
-
-    for part in range(HEADS_PER_STEP):
-        lanes = pl.ds(part * HEAD_SIZE, HEAD_SIZE)
-        rotate_rows(k_parts[part], 0, key_ref, lanes, cos_ref, sin_ref)
-        start = 0
-        for arrived in (passed_value, direct_value):
-            span = pl.ds(start, arrived.shape[1])
-            v_parts[part][span, pl.ds(0, HEAD_SIZE)] = jnp.where(
-                even, arrived[0, :, lanes], swapped_value[0, span, lanes]
+    fill_ones(v_parts)
+    copies = []
+    for group in range(KEY_VALUE_HEADS // HEADS_PER_STEP):
+        for part in range(HEADS_PER_STEP):
+            lanes = pl.ds((group * HEADS_PER_STEP + part) * HEAD_SIZE, HEAD_SIZE)
+            rotate_rows(k_parts[part], 0, key_ref, lanes, cos_ref, sin_ref)
+            start = 0
+            for arrived in (passed_value, direct_value):
+                span = pl.ds(start, arrived.shape[1])
+                v_parts[part][span, pl.ds(0, HEAD_SIZE)] = jnp.where(
+                    even, arrived[0, :, lanes], swapped_value[0, span, lanes]
+                )
+                start += arrived.shape[1]
+        query, mean, out = (
+            of_group(ref, group, HEADS_PER_STEP * GROUP) for ref in (q_ref, mean_ref, held)
+        )
+        join_heads(True, group, rows, *work, bias_ref, level_ref, mean, query, out, None)
+        copies.append(
+            pltpu.make_async_copy(
+                out, of_group(out_ref, group, HEADS_PER_STEP * GROUP), sem.at[group]
             )
-            start += arrived.shape[1]
-    join_heads(True, group, rows, *work, bias_ref, level_ref, mean_ref, q_ref, out_ref, None)
-
-
-def join(cosine, signed_sine, bias, level, mean, query, arrived, pages=None):
+        )
+        copies[-1].start()
+    for copy in copies:
+        copy.wait()
+
+
+def of_group(ref, group, heads):
+    lanes = pl.ds(group * heads * HEAD_SIZE, heads * HEAD_SIZE)
+    return ref.at[:, :, lanes] if len(ref.shape) == 3 else ref.at[:, lanes]
+
+
+def attend_last(cosine, signed_sine, bias, level, mean, query, arrived):
+    rows = query.shape[1]
+    operands = [cosine, signed_sine, bias, level, mean, query, *arrived]
+    return pl.pallas_call(
+        lambda *refs: last_kernel(rows, *refs),
+        in_specs=[pl.BlockSpec(memory_space=pltpu.VMEM)] * len(operands),
+        out_specs=pl.BlockSpec(memory_space=pl.ANY),
+        out_shape=jax.ShapeDtypeStruct(query.shape, jnp.bfloat16),
+        scratch_shapes=[
+            pltpu.VMEM(query.shape, jnp.bfloat16),
+            pltpu.SemaphoreType.DMA((KEY_VALUE_HEADS // HEADS_PER_STEP,)),
+            *work_shapes(rows, bias.shape[1]),
+        ],
+        compiler_params=pltpu.CompilerParams(vmem_limit_bytes=vmem_bytes(bias.shape[1])),
+        cost_estimate=JOIN_COST,
+        name="last",
+    )(*operands)
+
+
+def attend_far(cosine, signed_sine, bias, level, mean, query, arrived, pages):
     rows = query.shape[1]
     whole = lambda group: (0, 0)
     by_group = lambda group: (0, 0, group)
@@ -489,24 +521,20 @@
     ]
     operands = [cosine, signed_sine, bias, level, mean, query]
     scratch = work_shapes(rows, bias.shape[1])
-    if pages is None:
-        kernel = lambda *refs: last_kernel(rows, *refs)
-        out_specs, out_shape = wide, jax.ShapeDtypeStruct(query.shape, jnp.bfloat16)
-    else:
-        kernel = lambda *refs: far_kernel(rows, len(arrived) // 2, *refs)
-        groups = KEY_VALUE_HEADS // HEADS_PER_STEP
-        for first in (0, groups):
-            in_specs.append(
-                pl.BlockSpec(
-                    (*pages.shape[:2], HEADS_PER_STEP * HEAD_SIZE),
-                    lambda group, first=first: (0, 0, first + group),
-                )
+    kernel = lambda *refs: far_kernel(rows, len(arrived) // 2, *refs)
+    groups = KEY_VALUE_HEADS // HEADS_PER_STEP
+    for first in (0, groups):
+        in_specs.append(
+            pl.BlockSpec(
+                (*pages.shape[:2], HEADS_PER_STEP * HEAD_SIZE),
+                lambda group, first=first: (0, 0, first + group),
             )
-            operands.append(pages)
-        out_specs = [flat, level_spec]
-        out_shape = [
-            jax.ShapeDtypeStruct(array.shape, jnp.float32) for array in (mean, level)
-        ]
+        )
+        operands.append(pages)
+    out_specs = [flat, level_spec]
+    out_shape = [
+        jax.ShapeDtypeStruct(array.shape, jnp.float32) for array in (mean, level)
+    ]
     return pl.pallas_call(
         kernel,
         grid=(KEY_VALUE_HEADS // HEADS_PER_STEP,),
@@ -516,7 +544,7 @@
         scratch_shapes=scratch,
         compiler_params=pltpu.CompilerParams(vmem_limit_bytes=vmem_bytes(bias.shape[1])),
         cost_estimate=JOIN_COST,
-        name="last" if pages is None else "far",
+        name="far",
     )(*operands, *arrived)
 
 
@@ -575,11 +603,11 @@
     direct_value = lax.ppermute(
         later_values, "blk", [(j, j + 1) for j in range(1, blocks - 1, 2)]
     )
-    mean, level = join(
+    mean, level = attend_far(
         cos_far, sin_far, far_bias, level, mean, query, [*far[::2], *far[1::2]],
         pages=gather_pages(table, [(0, 0, own_shard), *shards]),
     )
-    result = join(
+    result = attend_last(
         cos_last, sin_last, last_bias, level, mean, query,
         [far_key, swapped_value, passed_value, direct_value],
     )

time: 41.1 us -> 40.5 us (0.985)
  Pallas kernels: 18.5 us -> 17.9 us
    pallas_call x2, Pallas kernels: 9.47 us -> 8.86 us  [the longest x1 5.25 us: attend_far(): pl.pallas_call(kernel, grid=(KEY_VALUE_HEADS // HEADS_PER_STEP,), in_spec...]
  transfers between devices with their start and end apart: 10 -> 10, of which waited for: 3 -> 3; matrix products, arithmetic and copies ran while one was open for 4% -> 4% of each run, Pallas kernels for 35% -> 36%
where the time goes in v3:
time: 40.5 us; the launch traced here: 39.7 us
  Pallas kernels  17.9 us (44%)
  starting transfers between devices  16.1 us (40%)
  waiting for transfers between devices  3.26 us (8%)
  local copies, waits for them, and re-layouts  0.86 us (2%)
  other arithmetic  0.82 us (2%)
  between operations  0.81 us (2%)
    ppermute x2, starting transfers between devices, shifted(): lax.ppermute(value, 'blk', [(source, source + steps) for source in range(...  6.96 us
    pallas_call x1, Pallas kernels, attend_far(): pl.pallas_call(kernel, grid=(KEY_VALUE_HEADS // HEADS_PER_STEP,), in_spec...  5.25 us
    pallas_call x1, Pallas kernels, attend_last(): pl.pallas_call(lambda *refs: last_kernel(rows, *refs), in_specs=[pl.Block...  3.61 us
    ppermute x1, starting transfers between devices, per_device(): lax.ppermute(swapped_value[:, :split], 'blk', [(j, j + 2) for j in range(...  3.48 us
    pallas_call x1, Pallas kernels, attend_own(): pl.pallas_call(lambda *refs: own_kernel(rows, *refs), grid=(KEY_VALUE_HEA...  2.79 us
    pallas_call x1, Pallas kernels, gather_pages(): pl.pallas_call(lambda *refs: gather_kernel(pool_rows, places, *refs), in_...  2.36 us
    ppermute x4, starting transfers between devices, swapped(): return lax.ppermute(shard, 'batch', [(c, c ^ bit) for c in range(count)])  2.23 us
    pallas_call x1, Pallas kernels, tables(): pl.pallas_call(lambda *refs: tables_kernel(rows, steps, segs, prefix_len,...  2.04 us
  transfers between devices with their start and end apart: 10, of which 3 were waited for; matrix products, arithmetic and copies ran while one was open for 4% of the time, Pallas kernels for 36%

profile of v3, /device:TPU:8, one launch (start us, length us, event | category | flops | bytes accessed | tf_op | source)
XLA Modules:
  0.0 39.7 jit_solution(10938947966652992933)
XLA Ops:
  0.6 3.5 %collective-permute-start.2 = (bf16[1,256,1024]{2,1,0:T(8,128)(2,1)}, bf16[1,256,1024]{2,1,0:T(8,128)(2,1)S(1)}, u32[]{:S(2)}, u32[]{:S(2)}) collective-permute-start(bf16[1,256,1024]{2,1,0:T(8,128)(2,1)} %refs_3_.1), channel_id=1, source_target_pairs={{0,8},{4,12},{8,16},{12,20},{16,24},{20,28},{1,9},{5,13},{9,17},{1... | collective-permute-start | bytes 1572872 | tf_op jit(solution)/shard_map/ppermute | solution.py:45
  4.1 0.1 collective-permute-start
  4.2 1.6 %collective-permute-start.1 = (bf16[8,16,2048]{2,1,0:T(8,128)(2,1)}, bf16[8,16,2048]{2,1,0:T(8,128)(2,1)S(1)}, u32[]{:S(2)}, u32[]{:S(2)}) collective-permute-start(bf16[8,16,2048]{2,1,0:T(8,128)(2,1)} %refs_5_.1), channel_id=1, source_target_pairs={{0,2},{1,3},{2,0},{3,1},{4,6},{5,7},{6,4},{7,5},{8,10},{9,11},{10,... | collective-permute-start | bytes 1572872 | tf_op jit(solution)/shard_map/ppermute | solution.py:555
  5.8 1.5 %collective-permute-start.3 = (bf16[1,256,1024]{2,1,0:T(8,128)(2,1)}, bf16[1,256,1024]{2,1,0:T(8,128)(2,1)S(1)}, u32[]{:S(2)}, u32[]{:S(2)}) collective-permute-start(bf16[1,256,1024]{2,1,0:T(8,128)(2,1)} %refs_4_.1), channel_id=1, source_target_pairs={{0,4},{4,0},{8,12},{12,8},{16,20},{20,16},{24,28},{28,24},{1,5},{5... | collective-permute-start | bytes 1572872 | tf_op jit(solution)/shard_map/ppermute | solution.py:583
  7.3 3.5 %collective-permute-start.6 = (bf16[1,256,1024]{2,1,0:T(8,128)(2,1)}, bf16[1,256,1024]{2,1,0:T(8,128)(2,1)S(1)}, u32[]{:S(2)}, u32[]{:S(2)}) collective-permute-start(bf16[1,256,1024]{2,1,0:T(8,128)(2,1)} %refs_4_.1), channel_id=1, source_target_pairs={{0,8},{4,12},{8,16},{12,20},{16,24},{20,28},{1,9},{5,13},{9,17},{1... | collective-permute-start | bytes 1572872 | tf_op jit(solution)/shard_map/ppermute | solution.py:45
  10.8 0.8 %reshape.15 = s32[56]{0:T(128)S(1)} reshape(s32[4,2,7]{2,1,0:T(2,128)} %bitcast.3) | data formatting | bytes 448 | tf_op jit(solution)/shard_map/reshape | solution.py:584
  11.5 0.8 %pad_add_fusion.refs_0_ = s32[65]{0:T(128)S(1)} fusion(s32[56]{0:T(128)S(1)} %reshape.15, s32[2]{0:T(128)} %bitcast.4, s32[7]{0:T(128)} %bitcast.5), kind=kLoop, calls=%fused_computation.1 | loop fusion | flops 130 | bytes 520 | tf_op jit(solution)/shard_map/concatenate | solution.py:584
  12.3 0.0 copy-start
  12.3 0.0 copy-start.1
  12.3 0.0 copy-start.2
  12.3 0.0 copy-start.3
  12.3 2.0 %tables.1 = (s32[14]{0:T(128)S(1)}, f32[256,128]{1,0:T(8,128)S(1)}, f32[256,128]{1,0:T(8,128)S(1)}, f32[256,128]{1,0:T(8,128)S(1)}, f32[256,128]{1,0:T(8,128)S(1...) custom-call(s32[65]{0:T(128)S(1)} %pad_add_fusion.refs_0_), custom_call_target="tpu_custom_call" | custom-call | flops 2000000000 | tf_op jit(solution)/shard_map/tables/pallas_call | solution.py:159
  14.4 0.0 copy-done
  14.4 0.0 copy-done.1
  14.4 0.0 copy-done.2
  14.4 0.0 copy-done.3
  14.4 1.8 %prepare.1 = (bf16[1,256,2048]{2,1,0:T(8,128)(2,1)S(1)}, bf16[1,256,1024]{2,1,0:T(8,128)(2,1)}, bf16[1,256,1024]{2,1,0:T(8,128)(2,1)S(1)}, bf16[1,256,1024]{2,1,0:T(8,128)(2,1)S(1)}, bf16[8,16,2048]{2,1,0:T(8,128)(2,1)S(1)}) custom-call(f32[256,128]{1,0:T(8,128)S(1)} %get-tuple-element.35.refs_0_, f32[256,128]{1,0:T(8,128)S(1)} %get-tuple-element.36.refs_1_, ...), custom_call_target="tpu_custom_call" | custom-call | tf_op jit(solution)/shard_map/prepare/pallas_call | solution.py:199
  16.2 2.8 %own.1 = (f32[256,2048]{1,0:T(8,128)S(1)}, f32[256,128]{1,0:T(8,128)S(1)}) custom-call(f32[256,256]{1,0:T(8,128)S(1)} %get-tuple-element.34.refs_0_, bf16[1,256,2048]{2,1,0:T(8,128)(2,1)S(1)} %get-tuple-element.37.refs_1_.refs_5_, bf16[1,256,1024]{2,1,0:T(8,128)(2,1)S(1)} %get-tuple-element.38.refs_2_, bf16[1,256,1024]{2,1,0:T(8,128)(2,1)S(1)} %get-tuple-element.39.refs_3_), custom_call_target="tpu_custom_call" | custom-call | tf_op jit(solution)/shard_map/own/pallas_call | solution.py:302
  19.0 0.0 collective-permute-done.2.refs_8_
  19.0 0.1 broadcast_select_fusion
  19.1 0.6 %collective-permute-start.7 = (bf16[1,256,1024]{2,1,0:T(8,128)(2,1)S(1)}, bf16[1,256,1024]{2,1,0:T(8,128)(2,1)S(1)}, u32[]{:S(2)}, u32[]{:S(2)}) collective-permute-start(bf16[1,256,1024]{2,1,0:T(8,128)(2,1)S(1)} %broadcast_select_fusion), channel_id=1, source_target_pairs={{0,4},{4,0},{8,12},{12,8},{16,20},{20,16},{24,28},{28,24},{1,5},{5... | collective-permute-start | bytes 1572872 | tf_op jit(solution)/shard_map/ppermute | solution.py:592
  19.7 0.0 collective-permute-done.refs_2_
  19.7 0.0 collective-permute-done.1.refs_3_
  19.7 0.3 collective-permute-done.3.refs_7_
  20.0 0.1 collective-permute-start.4
  20.1 0.5 %collective-permute-start.5 = (bf16[4,16,2048]{2,1,0:T(8,128)(2,1)S(1)}, bf16[4,16,2048]{2,1,0:T(8,128)(2,1)S(1)}, u32[]{:S(2)}, u32[]{:S(2)}) collective-permute-start(bf16[4,16,2048]{2,1,0:T(8,128)(2,1)S(1)} %get-tuple-element.54), channel_id=1, source_target_pairs={{0,1},{1,0},{2,3},{3,2},{4,5},{5,4},{6,7},{7,6},{8,9},{9,8},{10,11... | collective-permute-start | bytes 786440 | tf_op jit(solution)/shard_map/ppermute | solution.py:555
  20.6 3.5 %collective-permute-start.8 = (bf16[1,192,1024]{2,1,0:T(8,128)(2,1)S(1)}, bf16[1,192,1024]{2,1,0:T(8,128)(2,1)S(1)}, u32[]{:S(2)}, u32[]{:S(2)}) collective-permute-start(bf16[1,192,1024]{2,1,0:T(8,128)(2,1)S(1)} %slice.16), channel_id=1, source_target_pairs={{0,8},{8,16},{16,24},{1,9},{9,17},{17,25},{2,10},{10,18},{18,26},{... | collective-permute-start | bytes 1179656 | tf_op jit(solution)/shard_map/ppermute | solution.py:594
  24.1 0.0 collective-permute-done.4.refs_4_
  24.2 0.0 collective-permute-done.5.refs_5_
  24.2 1.3 %collective-permute-start.9 = (bf16[1,64,1024]{2,1,0:T(8,128)(2,1)S(1)}, bf16[1,64,1024]{2,1,0:T(8,128)(2,1)S(1)}, u32[]{:S(2)}, u32[]{:S(2)}) collective-permute-start(bf16[1,64,1024]{2,1,0:T(8,128)(2,1)S(1)} %slice.14), channel_id=1, source_target_pairs={{4,8},{12,16},{20,24},{5,9},{13,17},{21,25},{6,10},{14,18},{22,26}... | collective-permute-start | bytes 393224 | tf_op jit(solution)/shard_map/ppermute | solution.py:603
  25.5 2.4 %gather.1.refs_6_.refs_7_ = bf16[14,16,2048]{2,1,0:T(8,128)(2,1)S(1)} custom-call(s32[14]{0:T(128)S(1)} %get-tuple-element.42.refs_0_, bf16[8,16,2048]{2,1,0:T(8,128)(2,1)S(1)} %get-tuple-element.43.refs_1_, bf16[8,16,2048]{2,1,0:T(8,128)(2,1)S(1)} %collective-permute-done.refs_2_, bf16[8,16,2048]{2,1,0:T(8,128)(2,1)S(1)} %collective-permute-done.1.refs_3_, ...), custom_call_target="tpu_custom_call" | custom-call | tf_op jit(solution)/shard_map/gather/pallas_call | solution.py:351
  27.8 0.9 %collective-permute-done.6.refs_9_ = bf16[1,256,1024]{2,1,0:T(8,128)(2,1)S(1)} collective-permute-done((bf16[1,256,1024]{2,1,0:T(8,128)(2,1)}, bf16[1,256,1024]{2,1,0:T(8,128)(2,1)S(1)}, u32[]{:S(2)}, u32[]{:S(2)}) %collective-permute-start.6) | collective-permute-done | bytes 524320 | tf_op jit(solution)/shard_map/ppermute | solution.py:45
  28.8 5.2 %far.1 = (f32[256,2048]{1,0:T(8,128)S(1)}, f32[256,128]{1,0:T(8,128)S(1)}) custom-call(f32[256,128]{1,0:T(8,128)S(1)} %get-tuple-element.31.refs_0_, f32[256,128]{1,0:T(8,128)S(1)} %get-tuple-element.32.refs_1_, f32[256,512]{1,0:T(8,128)S(1)} %get-tuple-element.33.refs_2_, f32[256,128]{1,0:T(8,128)S(1)} %get-tuple-element.40.refs_3_, ...), custom_call_target="tpu_custom_call" | custom-call | tf_op jit(solution)/shard_map/far/pallas_call | solution.py:538
  34.0 0.0 collective-permute-done.9.refs_9_
  34.0 2.0 %collective-permute-done.8.refs_8_ = bf16[1,192,1024]{2,1,0:T(8,128)(2,1)S(1)} collective-permute-done((bf16[1,192,1024]{2,1,0:T(8,128)(2,1)S(1)}, bf16[1,192,1024]{2,1,0:T(8,128)(2,1)S(1)}, u32[]{:S(2)}, u32[]{:S(2)}) %collective-permute-start.8) | collective-permute-done | bytes 393248 | tf_op jit(solution)/shard_map/ppermute | solution.py:594
  36.1 0.0 collective-permute-done.7.refs_6_
  36.1 3.6 %last.1 = bf16[1,256,2048]{2,1,0:T(8,128)(2,1)} custom-call(f32[256,128]{1,0:T(8,128)S(1)} %get-tuple-element.28.refs_0_, f32[256,128]{1,0:T(8,128)S(1)} %get-tuple-element.29.refs_1_, f32[256,256]{1,0:T(8,128)S(1)} %get-tuple-element.30.refs_2_, f32[256,128]{1,0:T(8,128)S(1)} %get-tuple-element.50.refs_3_, f32[256,2048]{1,0:T(8,128)S(1)} %get-tuple-element.51.refs_4_, ...), custom_call_target="tpu_custom_call" | custom-call | tf_op jit(solution)/shard_map/last/pallas_call | solution.py:492
  (3 shorter events, 0.1 us)
Async XLA Ops:
  0.6 18.4 %collective-permute-start.2 = (bf16[1,256,1024]{2,1,0:T(8,128)(2,1)}, bf16[1,256,1024]{2,1,0:T(8,128)(2,1)S(1)}, u32[]{:S(2)}, u32[]{:S(2)}) collective-permute-start(bf16[1,256,1024]{2,1,0:T(8,128)(2,1)} %refs_3_.1), channel_id=1, source_target_pairs={{0,8},{4,12},{8,16},{12,20},{16,24},{20,28},{1,9},{5,13},{9,17},{1... | collective-permute-start | bytes 1572872 | tf_op jit(solution)/shard_map/ppermute | solution.py:45
  4.1 15.6 %collective-permute-start = (bf16[8,16,2048]{2,1,0:T(8,128)(2,1)}, bf16[8,16,2048]{2,1,0:T(8,128)(2,1)S(1)}, u32[]{:S(2)}, u32[]{:S(2)}) collective-permute-start(bf16[8,16,2048]{2,1,0:T(8,128)(2,1)} %refs_5_.1), channel_id=1, source_target_pairs={{0,1},{1,0},{2,3},{3,2},{4,5},{5,4},{6,7},{7,6},{8,9},{9,8},{10,11... | collective-permute-start | bytes 1572872 | tf_op jit(solution)/shard_map/ppermute | solution.py:555
  4.2 15.5 %collective-permute-start.1 = (bf16[8,16,2048]{2,1,0:T(8,128)(2,1)}, bf16[8,16,2048]{2,1,0:T(8,128)(2,1)S(1)}, u32[]{:S(2)}, u32[]{:S(2)}) collective-permute-start(bf16[8,16,2048]{2,1,0:T(8,128)(2,1)} %refs_5_.1), channel_id=1, source_target_pairs={{0,2},{1,3},{2,0},{3,1},{4,6},{5,7},{6,4},{7,5},{8,10},{9,11},{10,... | collective-permute-start | bytes 1572872 | tf_op jit(solution)/shard_map/ppermute | solution.py:555
  5.8 14.2 %collective-permute-start.3 = (bf16[1,256,1024]{2,1,0:T(8,128)(2,1)}, bf16[1,256,1024]{2,1,0:T(8,128)(2,1)S(1)}, u32[]{:S(2)}, u32[]{:S(2)}) collective-permute-start(bf16[1,256,1024]{2,1,0:T(8,128)(2,1)} %refs_4_.1), channel_id=1, source_target_pairs={{0,4},{4,0},{8,12},{12,8},{16,20},{20,16},{24,28},{28,24},{1,5},{5... | collective-permute-start | bytes 1572872 | tf_op jit(solution)/shard_map/ppermute | solution.py:583
  7.3 21.5 %collective-permute-start.6 = (bf16[1,256,1024]{2,1,0:T(8,128)(2,1)}, bf16[1,256,1024]{2,1,0:T(8,128)(2,1)S(1)}, u32[]{:S(2)}, u32[]{:S(2)}) collective-permute-start(bf16[1,256,1024]{2,1,0:T(8,128)(2,1)} %refs_4_.1), channel_id=1, source_target_pairs={{0,8},{4,12},{8,16},{12,20},{16,24},{20,28},{1,9},{5,13},{9,17},{1... | collective-permute-start | bytes 1572872 | tf_op jit(solution)/shard_map/ppermute | solution.py:45
  12.3 2.1 %copy-start = (bf16[1,256,1024]{2,1,0:T(8,128)(2,1)S(1)}, bf16[1,256,1024]{2,1,0:T(8,128)(2,1)}, u32[]{:S(2)}) copy-start(bf16[1,256,1024]{2,1,0:T(8,128)(2,1)} %refs_3_.1) | copy-start | bytes 1572868
  12.3 2.1 %copy-start.1 = (bf16[1,256,2048]{2,1,0:T(8,128)(2,1)S(1)}, bf16[1,256,2048]{2,1,0:T(8,128)(2,1)}, u32[]{:S(2)}) copy-start(bf16[1,256,2048]{2,1,0:T(8,128)(2,1)} %refs_2_.1) | copy-start | bytes 3145732
  12.3 2.1 %copy-start.2 = (bf16[1,256,1024]{2,1,0:T(8,128)(2,1)S(1)}, bf16[1,256,1024]{2,1,0:T(8,128)(2,1)}, u32[]{:S(2)}) copy-start(bf16[1,256,1024]{2,1,0:T(8,128)(2,1)} %refs_4_.1) | copy-start | bytes 1572868
  12.3 2.1 %copy-start.3 = (bf16[8,16,2048]{2,1,0:T(8,128)(2,1)S(1)}, bf16[8,16,2048]{2,1,0:T(8,128)(2,1)}, u32[]{:S(2)}) copy-start(bf16[8,16,2048]{2,1,0:T(8,128)(2,1)} %refs_5_.1) | copy-start | bytes 1572868
  19.1 17.0 %collective-permute-start.7 = (bf16[1,256,1024]{2,1,0:T(8,128)(2,1)S(1)}, bf16[1,256,1024]{2,1,0:T(8,128)(2,1)S(1)}, u32[]{:S(2)}, u32[]{:S(2)}) collective-permute-start(bf16[1,256,1024]{2,1,0:T(8,128)(2,1)S(1)} %broadcast_select_fusion), channel_id=1, source_target_pairs={{0,4},{4,0},{8,12},{12,8},{16,20},{20,16},{24,28},{28,24},{1,5},{5... | collective-permute-start | bytes 1572872 | tf_op jit(solution)/shard_map/ppermute | solution.py:592
  20.0 4.1 %collective-permute-start.4 = (bf16[4,16,2048]{2,1,0:T(8,128)(2,1)S(1)}, bf16[4,16,2048]{2,1,0:T(8,128)(2,1)S(1)}, u32[]{:S(2)}, u32[]{:S(2)}) collective-permute-start(bf16[4,16,2048]{2,1,0:T(8,128)(2,1)S(1)} %get-tuple-element.55), channel_id=1, source_target_pairs={{0,1},{1,0},{2,3},{3,2},{4,5},{5,4},{6,7},{7,6},{8,9},{9,8},{10,11... | collective-permute-start | bytes 786440 | tf_op jit(solution)/shard_map/ppermute | solution.py:555
  20.1 4.1 %collective-permute-start.5 = (bf16[4,16,2048]{2,1,0:T(8,128)(2,1)S(1)}, bf16[4,16,2048]{2,1,0:T(8,128)(2,1)S(1)}, u32[]{:S(2)}, u32[]{:S(2)}) collective-permute-start(bf16[4,16,2048]{2,1,0:T(8,128)(2,1)S(1)} %get-tuple-element.54), channel_id=1, source_target_pairs={{0,1},{1,0},{2,3},{3,2},{4,5},{5,4},{6,7},{7,6},{8,9},{9,8},{10,11... | collective-permute-start | bytes 786440 | tf_op jit(solution)/shard_map/ppermute | solution.py:555
  20.6 15.4 %collective-permute-start.8 = (bf16[1,192,1024]{2,1,0:T(8,128)(2,1)S(1)}, bf16[1,192,1024]{2,1,0:T(8,128)(2,1)S(1)}, u32[]{:S(2)}, u32[]{:S(2)}) collective-permute-start(bf16[1,192,1024]{2,1,0:T(8,128)(2,1)S(1)} %slice.16), channel_id=1, source_target_pairs={{0,8},{8,16},{16,24},{1,9},{9,17},{17,25},{2,10},{10,18},{18,26},{... | collective-permute-start | bytes 1179656 | tf_op jit(solution)/shard_map/ppermute | solution.py:594
  24.2 9.9 %collective-permute-start.9 = (bf16[1,64,1024]{2,1,0:T(8,128)(2,1)S(1)}, bf16[1,64,1024]{2,1,0:T(8,128)(2,1)S(1)}, u32[]{:S(2)}, u32[]{:S(2)}) collective-permute-start(bf16[1,64,1024]{2,1,0:T(8,128)(2,1)S(1)} %slice.14), channel_id=1, source_target_pairs={{4,8},{12,16},{20,24},{5,9},{13,17},{21,25},{6,10},{14,18},{22,26}... | collective-permute-start | bytes 393224 | tf_op jit(solution)/shard_map/ppermute | solution.py:603

commit v4 on v3

--- a/solution.py
+++ b/solution.py
@@ -590,7 +590,7 @@
     )
     to_swap = jnp.where(even, keys, far[0])
     far_key = lax.ppermute(to_swap, "blk", swap)
-    split = values.shape[1] * 3 // 4
+    split = values.shape[1] * 11 // 16
     passed_value = lax.ppermute(
         swapped_value[:, :split], "blk", [(j, j + 2) for j in range(0, blocks - 2, 2)]
     )

time: 40.5 us -> 40 us (0.988); the launches traced: 39.7 us -> 39.7 us
    ppermute x1, waiting for transfers between devices: 0.01 us -> 0.75 us  [per_device(): far_key = lax.ppermute(to_swap, 'blk', swap)]
    ppermute x1, waiting for transfers between devices: 2.01 us -> 1.32 us  [per_device(): lax.ppermute(swapped_value[:, :split], 'blk', [(j, j + 2) for j in range(...]
  transfers between devices with their start and end apart: 10 -> 10, of which waited for: 3 -> 4; matrix products, arithmetic and copies ran while one was open for 4% -> 4% of each run, Pallas kernels for 36% -> 36%
where the time goes in v4:
time: 40 us; the launch traced here: 39.7 us
  Pallas kernels  17.9 us (45%)
  starting transfers between devices  16.1 us (40%)
  waiting for transfers between devices  3.31 us (8%)
  local copies, waits for them, and re-layouts  0.86 us (2%)
  other arithmetic  0.82 us (2%)
  between operations  0.8 us (2%)
    ppermute x2, starting transfers between devices, shifted(): lax.ppermute(value, 'blk', [(source, source + steps) for source in range(...  6.96 us
    pallas_call x1, Pallas kernels, attend_far(): pl.pallas_call(kernel, grid=(KEY_VALUE_HEADS // HEADS_PER_STEP,), in_spec...  5.25 us
    pallas_call x1, Pallas kernels, attend_last(): pl.pallas_call(lambda *refs: last_kernel(rows, *refs), in_specs=[pl.Block...  3.6 us
    ppermute x1, starting transfers between devices, per_device(): lax.ppermute(swapped_value[:, :split], 'blk', [(j, j + 2) for j in range(...  3.48 us
    pallas_call x1, Pallas kernels, attend_own(): pl.pallas_call(lambda *refs: own_kernel(rows, *refs), grid=(KEY_VALUE_HEA...  2.79 us
    pallas_call x1, Pallas kernels, gather_pages(): pl.pallas_call(lambda *refs: gather_kernel(pool_rows, places, *refs), in_...  2.36 us
    ppermute x4, starting transfers between devices, swapped(): return lax.ppermute(shard, 'batch', [(c, c ^ bit) for c in range(count)])  2.23 us
    pallas_call x1, Pallas kernels, tables(): pl.pallas_call(lambda *refs: tables_kernel(rows, steps, segs, prefix_len,...  2.04 us
  transfers between devices with their start and end apart: 10, of which 4 were waited for; matrix products, arithmetic and copies ran while one was open for 4% of the time, Pallas kernels for 36%

profile of v4, /device:TPU:8, one launch (start us, length us, event | category | flops | bytes accessed | tf_op | source)
XLA Modules:
  0.0 39.7 jit_solution(8580569078408816228)
XLA Ops:
  0.6 3.5 %collective-permute-start.2 = (bf16[1,256,1024]{2,1,0:T(8,128)(2,1)}, bf16[1,256,1024]{2,1,0:T(8,128)(2,1)S(1)}, u32[]{:S(2)}, u32[]{:S(2)}) collective-permute-start(bf16[1,256,1024]{2,1,0:T(8,128)(2,1)} %refs_3_.1), channel_id=1, source_target_pairs={{0,8},{4,12},{8,16},{12,20},{16,24},{20,28},{1,9},{5,13},{9,17},{1... | collective-permute-start | bytes 1572872 | tf_op jit(solution)/shard_map/ppermute | solution.py:45
  4.1 0.1 collective-permute-start
  4.2 1.6 %collective-permute-start.1 = (bf16[8,16,2048]{2,1,0:T(8,128)(2,1)}, bf16[8,16,2048]{2,1,0:T(8,128)(2,1)S(1)}, u32[]{:S(2)}, u32[]{:S(2)}) collective-permute-start(bf16[8,16,2048]{2,1,0:T(8,128)(2,1)} %refs_5_.1), channel_id=1, source_target_pairs={{0,2},{1,3},{2,0},{3,1},{4,6},{5,7},{6,4},{7,5},{8,10},{9,11},{10,... | collective-permute-start | bytes 1572872 | tf_op jit(solution)/shard_map/ppermute | solution.py:555
  5.8 1.5 %collective-permute-start.3 = (bf16[1,256,1024]{2,1,0:T(8,128)(2,1)}, bf16[1,256,1024]{2,1,0:T(8,128)(2,1)S(1)}, u32[]{:S(2)}, u32[]{:S(2)}) collective-permute-start(bf16[1,256,1024]{2,1,0:T(8,128)(2,1)} %refs_4_.1), channel_id=1, source_target_pairs={{0,4},{4,0},{8,12},{12,8},{16,20},{20,16},{24,28},{28,24},{1,5},{5... | collective-permute-start | bytes 1572872 | tf_op jit(solution)/shard_map/ppermute | solution.py:583
  7.3 3.5 %collective-permute-start.6 = (bf16[1,256,1024]{2,1,0:T(8,128)(2,1)}, bf16[1,256,1024]{2,1,0:T(8,128)(2,1)S(1)}, u32[]{:S(2)}, u32[]{:S(2)}) collective-permute-start(bf16[1,256,1024]{2,1,0:T(8,128)(2,1)} %refs_4_.1), channel_id=1, source_target_pairs={{0,8},{4,12},{8,16},{12,20},{16,24},{20,28},{1,9},{5,13},{9,17},{1... | collective-permute-start | bytes 1572872 | tf_op jit(solution)/shard_map/ppermute | solution.py:45
  10.8 0.8 %reshape.15 = s32[56]{0:T(128)S(1)} reshape(s32[4,2,7]{2,1,0:T(2,128)} %bitcast.3) | data formatting | bytes 448 | tf_op jit(solution)/shard_map/reshape | solution.py:584
  11.5 0.8 %pad_add_fusion.refs_0_ = s32[65]{0:T(128)S(1)} fusion(s32[56]{0:T(128)S(1)} %reshape.15, s32[2]{0:T(128)} %bitcast.4, s32[7]{0:T(128)} %bitcast.5), kind=kLoop, calls=%fused_computation.1 | loop fusion | flops 130 | bytes 520 | tf_op jit(solution)/shard_map/concatenate | solution.py:584
  12.3 0.0 copy-start
  12.3 0.0 copy-start.1
  12.3 0.0 copy-start.2
  12.3 0.0 copy-start.3
  12.3 2.0 %tables.1 = (s32[14]{0:T(128)S(1)}, f32[256,128]{1,0:T(8,128)S(1)}, f32[256,128]{1,0:T(8,128)S(1)}, f32[256,128]{1,0:T(8,128)S(1)}, f32[256,128]{1,0:T(8,128)S(1...) custom-call(s32[65]{0:T(128)S(1)} %pad_add_fusion.refs_0_), custom_call_target="tpu_custom_call" | custom-call | flops 2000000000 | tf_op jit(solution)/shard_map/tables/pallas_call | solution.py:159
  14.4 0.0 copy-done
  14.4 0.0 copy-done.1
  14.4 0.0 copy-done.2
  14.4 0.0 copy-done.3
  14.4 1.8 %prepare.1 = (bf16[1,256,2048]{2,1,0:T(8,128)(2,1)S(1)}, bf16[1,256,1024]{2,1,0:T(8,128)(2,1)}, bf16[1,256,1024]{2,1,0:T(8,128)(2,1)S(1)}, bf16[1,256,1024]{2,1,0:T(8,128)(2,1)S(1)}, bf16[8,16,2048]{2,1,0:T(8,128)(2,1)S(1)}) custom-call(f32[256,128]{1,0:T(8,128)S(1)} %get-tuple-element.35.refs_0_, f32[256,128]{1,0:T(8,128)S(1)} %get-tuple-element.36.refs_1_, ...), custom_call_target="tpu_custom_call" | custom-call | tf_op jit(solution)/shard_map/prepare/pallas_call | solution.py:199
  16.2 2.8 %own.1 = (f32[256,2048]{1,0:T(8,128)S(1)}, f32[256,128]{1,0:T(8,128)S(1)}) custom-call(f32[256,256]{1,0:T(8,128)S(1)} %get-tuple-element.34.refs_0_, bf16[1,256,2048]{2,1,0:T(8,128)(2,1)S(1)} %get-tuple-element.37.refs_1_.refs_5_, bf16[1,256,1024]{2,1,0:T(8,128)(2,1)S(1)} %get-tuple-element.38.refs_2_, bf16[1,256,1024]{2,1,0:T(8,128)(2,1)S(1)} %get-tuple-element.39.refs_3_), custom_call_target="tpu_custom_call" | custom-call | tf_op jit(solution)/shard_map/own/pallas_call | solution.py:302
  19.0 0.0 collective-permute-done.2.refs_8_
  19.0 0.1 broadcast_select_fusion
  19.1 0.6 %collective-permute-start.7 = (bf16[1,256,1024]{2,1,0:T(8,128)(2,1)S(1)}, bf16[1,256,1024]{2,1,0:T(8,128)(2,1)S(1)}, u32[]{:S(2)}, u32[]{:S(2)}) collective-permute-start(bf16[1,256,1024]{2,1,0:T(8,128)(2,1)S(1)} %broadcast_select_fusion), channel_id=1, source_target_pairs={{0,4},{4,0},{8,12},{12,8},{16,20},{20,16},{24,28},{28,24},{1,5},{5... | collective-permute-start | bytes 1572872 | tf_op jit(solution)/shard_map/ppermute | solution.py:592
  19.7 0.0 collective-permute-done.refs_2_
  19.7 0.0 collective-permute-done.1.refs_3_
  19.7 0.3 collective-permute-done.3.refs_7_
  20.0 0.1 collective-permute-start.4
  20.1 0.5 %collective-permute-start.5 = (bf16[4,16,2048]{2,1,0:T(8,128)(2,1)S(1)}, bf16[4,16,2048]{2,1,0:T(8,128)(2,1)S(1)}, u32[]{:S(2)}, u32[]{:S(2)}) collective-permute-start(bf16[4,16,2048]{2,1,0:T(8,128)(2,1)S(1)} %get-tuple-element.54), channel_id=1, source_target_pairs={{0,1},{1,0},{2,3},{3,2},{4,5},{5,4},{6,7},{7,6},{8,9},{9,8},{10,11... | collective-permute-start | bytes 786440 | tf_op jit(solution)/shard_map/ppermute | solution.py:555
  20.6 3.5 %collective-permute-start.8 = (bf16[1,176,1024]{2,1,0:T(8,128)(2,1)S(1)}, bf16[1,176,1024]{2,1,0:T(8,128)(2,1)S(1)}, u32[]{:S(2)}, u32[]{:S(2)}) collective-permute-start(bf16[1,176,1024]{2,1,0:T(8,128)(2,1)S(1)} %slice.16), channel_id=1, source_target_pairs={{0,8},{8,16},{16,24},{1,9},{9,17},{17,25},{2,10},{10,18},{18,26},{... | collective-permute-start | bytes 1081352 | tf_op jit(solution)/shard_map/ppermute | solution.py:594
  24.1 0.0 collective-permute-done.4.refs_4_
  24.2 0.0 collective-permute-done.5.refs_5_
  24.2 1.3 %collective-permute-start.9 = (bf16[1,80,1024]{2,1,0:T(8,128)(2,1)S(1)}, bf16[1,80,1024]{2,1,0:T(8,128)(2,1)S(1)}, u32[]{:S(2)}, u32[]{:S(2)}) collective-permute-start(bf16[1,80,1024]{2,1,0:T(8,128)(2,1)S(1)} %slice.14), channel_id=1, source_target_pairs={{4,8},{12,16},{20,24},{5,9},{13,17},{21,25},{6,10},{14,18},{22,26}... | collective-permute-start | bytes 491528 | tf_op jit(solution)/shard_map/ppermute | solution.py:603
  25.5 2.4 %gather.1.refs_6_.refs_7_ = bf16[14,16,2048]{2,1,0:T(8,128)(2,1)S(1)} custom-call(s32[14]{0:T(128)S(1)} %get-tuple-element.42.refs_0_, bf16[8,16,2048]{2,1,0:T(8,128)(2,1)S(1)} %get-tuple-element.43.refs_1_, bf16[8,16,2048]{2,1,0:T(8,128)(2,1)S(1)} %collective-permute-done.refs_2_, bf16[8,16,2048]{2,1,0:T(8,128)(2,1)S(1)} %collective-permute-done.1.refs_3_, ...), custom_call_target="tpu_custom_call" | custom-call | tf_op jit(solution)/shard_map/gather/pallas_call | solution.py:351
  27.8 0.9 %collective-permute-done.6.refs_9_ = bf16[1,256,1024]{2,1,0:T(8,128)(2,1)S(1)} collective-permute-done((bf16[1,256,1024]{2,1,0:T(8,128)(2,1)}, bf16[1,256,1024]{2,1,0:T(8,128)(2,1)S(1)}, u32[]{:S(2)}, u32[]{:S(2)}) %collective-permute-start.6) | collective-permute-done | bytes 524320 | tf_op jit(solution)/shard_map/ppermute | solution.py:45
  28.8 5.2 %far.1 = (f32[256,2048]{1,0:T(8,128)S(1)}, f32[256,128]{1,0:T(8,128)S(1)}) custom-call(f32[256,128]{1,0:T(8,128)S(1)} %get-tuple-element.31.refs_0_, f32[256,128]{1,0:T(8,128)S(1)} %get-tuple-element.32.refs_1_, f32[256,512]{1,0:T(8,128)S(1)} %get-tuple-element.33.refs_2_, f32[256,128]{1,0:T(8,128)S(1)} %get-tuple-element.40.refs_3_, ...), custom_call_target="tpu_custom_call" | custom-call | tf_op jit(solution)/shard_map/far/pallas_call | solution.py:538
  34.0 1.3 %collective-permute-done.8.refs_8_ = bf16[1,176,1024]{2,1,0:T(8,128)(2,1)S(1)} collective-permute-done((bf16[1,176,1024]{2,1,0:T(8,128)(2,1)S(1)}, bf16[1,176,1024]{2,1,0:T(8,128)(2,1)S(1)}, u32[]{:S(2)}, u32[]{:S(2)}) %collective-permute-start.8) | collective-permute-done | bytes 360480 | tf_op jit(solution)/shard_map/ppermute | solution.py:594
  35.4 0.0 collective-permute-done.9.refs_9_
  35.4 0.7 %collective-permute-done.7.refs_6_ = bf16[1,256,1024]{2,1,0:T(8,128)(2,1)S(1)} collective-permute-done((bf16[1,256,1024]{2,1,0:T(8,128)(2,1)S(1)}, bf16[1,256,1024]{2,1,0:T(8,128)(2,1)S(1)}, u32[]{:S(2)}, u32[]{:S(2)}) %collective-permute-start.7) | collective-permute-done | bytes 524320 | tf_op jit(solution)/shard_map/ppermute | solution.py:592
  36.1 3.6 %last.1 = bf16[1,256,2048]{2,1,0:T(8,128)(2,1)} custom-call(f32[256,128]{1,0:T(8,128)S(1)} %get-tuple-element.28.refs_0_, f32[256,128]{1,0:T(8,128)S(1)} %get-tuple-element.29.refs_1_, f32[256,256]{1,0:T(8,128)S(1)} %get-tuple-element.30.refs_2_, f32[256,128]{1,0:T(8,128)S(1)} %get-tuple-element.50.refs_3_, f32[256,2048]{1,0:T(8,128)S(1)} %get-tuple-element.51.refs_4_, ...), custom_call_target="tpu_custom_call" | custom-call | tf_op jit(solution)/shard_map/last/pallas_call | solution.py:492
  (3 shorter events, 0.1 us)
Async XLA Ops:
  0.6 18.4 %collective-permute-start.2 = (bf16[1,256,1024]{2,1,0:T(8,128)(2,1)}, bf16[1,256,1024]{2,1,0:T(8,128)(2,1)S(1)}, u32[]{:S(2)}, u32[]{:S(2)}) collective-permute-start(bf16[1,256,1024]{2,1,0:T(8,128)(2,1)} %refs_3_.1), channel_id=1, source_target_pairs={{0,8},{4,12},{8,16},{12,20},{16,24},{20,28},{1,9},{5,13},{9,17},{1... | collective-permute-start | bytes 1572872 | tf_op jit(solution)/shard_map/ppermute | solution.py:45
  4.1 15.6 %collective-permute-start = (bf16[8,16,2048]{2,1,0:T(8,128)(2,1)}, bf16[8,16,2048]{2,1,0:T(8,128)(2,1)S(1)}, u32[]{:S(2)}, u32[]{:S(2)}) collective-permute-start(bf16[8,16,2048]{2,1,0:T(8,128)(2,1)} %refs_5_.1), channel_id=1, source_target_pairs={{0,1},{1,0},{2,3},{3,2},{4,5},{5,4},{6,7},{7,6},{8,9},{9,8},{10,11... | collective-permute-start | bytes 1572872 | tf_op jit(solution)/shard_map/ppermute | solution.py:555
  4.2 15.5 %collective-permute-start.1 = (bf16[8,16,2048]{2,1,0:T(8,128)(2,1)}, bf16[8,16,2048]{2,1,0:T(8,128)(2,1)S(1)}, u32[]{:S(2)}, u32[]{:S(2)}) collective-permute-start(bf16[8,16,2048]{2,1,0:T(8,128)(2,1)} %refs_5_.1), channel_id=1, source_target_pairs={{0,2},{1,3},{2,0},{3,1},{4,6},{5,7},{6,4},{7,5},{8,10},{9,11},{10,... | collective-permute-start | bytes 1572872 | tf_op jit(solution)/shard_map/ppermute | solution.py:555
  5.8 14.2 %collective-permute-start.3 = (bf16[1,256,1024]{2,1,0:T(8,128)(2,1)}, bf16[1,256,1024]{2,1,0:T(8,128)(2,1)S(1)}, u32[]{:S(2)}, u32[]{:S(2)}) collective-permute-start(bf16[1,256,1024]{2,1,0:T(8,128)(2,1)} %refs_4_.1), channel_id=1, source_target_pairs={{0,4},{4,0},{8,12},{12,8},{16,20},{20,16},{24,28},{28,24},{1,5},{5... | collective-permute-start | bytes 1572872 | tf_op jit(solution)/shard_map/ppermute | solution.py:583
  7.3 21.5 %collective-permute-start.6 = (bf16[1,256,1024]{2,1,0:T(8,128)(2,1)}, bf16[1,256,1024]{2,1,0:T(8,128)(2,1)S(1)}, u32[]{:S(2)}, u32[]{:S(2)}) collective-permute-start(bf16[1,256,1024]{2,1,0:T(8,128)(2,1)} %refs_4_.1), channel_id=1, source_target_pairs={{0,8},{4,12},{8,16},{12,20},{16,24},{20,28},{1,9},{5,13},{9,17},{1... | collective-permute-start | bytes 1572872 | tf_op jit(solution)/shard_map/ppermute | solution.py:45
  12.3 2.1 %copy-start = (bf16[1,256,1024]{2,1,0:T(8,128)(2,1)S(1)}, bf16[1,256,1024]{2,1,0:T(8,128)(2,1)}, u32[]{:S(2)}) copy-start(bf16[1,256,1024]{2,1,0:T(8,128)(2,1)} %refs_3_.1) | copy-start | bytes 1572868
  12.3 2.1 %copy-start.1 = (bf16[1,256,2048]{2,1,0:T(8,128)(2,1)S(1)}, bf16[1,256,2048]{2,1,0:T(8,128)(2,1)}, u32[]{:S(2)}) copy-start(bf16[1,256,2048]{2,1,0:T(8,128)(2,1)} %refs_2_.1) | copy-start | bytes 3145732
  12.3 2.1 %copy-start.2 = (bf16[1,256,1024]{2,1,0:T(8,128)(2,1)S(1)}, bf16[1,256,1024]{2,1,0:T(8,128)(2,1)}, u32[]{:S(2)}) copy-start(bf16[1,256,1024]{2,1,0:T(8,128)(2,1)} %refs_4_.1) | copy-start | bytes 1572868
  12.3 2.1 %copy-start.3 = (bf16[8,16,2048]{2,1,0:T(8,128)(2,1)S(1)}, bf16[8,16,2048]{2,1,0:T(8,128)(2,1)}, u32[]{:S(2)}) copy-start(bf16[8,16,2048]{2,1,0:T(8,128)(2,1)} %refs_5_.1) | copy-start | bytes 1572868
  19.1 17.0 %collective-permute-start.7 = (bf16[1,256,1024]{2,1,0:T(8,128)(2,1)S(1)}, bf16[1,256,1024]{2,1,0:T(8,128)(2,1)S(1)}, u32[]{:S(2)}, u32[]{:S(2)}) collective-permute-start(bf16[1,256,1024]{2,1,0:T(8,128)(2,1)S(1)} %broadcast_select_fusion), channel_id=1, source_target_pairs={{0,4},{4,0},{8,12},{12,8},{16,20},{20,16},{24,28},{28,24},{1,5},{5... | collective-permute-start | bytes 1572872 | tf_op jit(solution)/shard_map/ppermute | solution.py:592
  20.0 4.1 %collective-permute-start.4 = (bf16[4,16,2048]{2,1,0:T(8,128)(2,1)S(1)}, bf16[4,16,2048]{2,1,0:T(8,128)(2,1)S(1)}, u32[]{:S(2)}, u32[]{:S(2)}) collective-permute-start(bf16[4,16,2048]{2,1,0:T(8,128)(2,1)S(1)} %get-tuple-element.55), channel_id=1, source_target_pairs={{0,1},{1,0},{2,3},{3,2},{4,5},{5,4},{6,7},{7,6},{8,9},{9,8},{10,11... | collective-permute-start | bytes 786440 | tf_op jit(solution)/shard_map/ppermute | solution.py:555
  20.1 4.1 %collective-permute-start.5 = (bf16[4,16,2048]{2,1,0:T(8,128)(2,1)S(1)}, bf16[4,16,2048]{2,1,0:T(8,128)(2,1)S(1)}, u32[]{:S(2)}, u32[]{:S(2)}) collective-permute-start(bf16[4,16,2048]{2,1,0:T(8,128)(2,1)S(1)} %get-tuple-element.54), channel_id=1, source_target_pairs={{0,1},{1,0},{2,3},{3,2},{4,5},{5,4},{6,7},{7,6},{8,9},{9,8},{10,11... | collective-permute-start | bytes 786440 | tf_op jit(solution)/shard_map/ppermute | solution.py:555
  20.6 14.7 %collective-permute-start.8 = (bf16[1,176,1024]{2,1,0:T(8,128)(2,1)S(1)}, bf16[1,176,1024]{2,1,0:T(8,128)(2,1)S(1)}, u32[]{:S(2)}, u32[]{:S(2)}) collective-permute-start(bf16[1,176,1024]{2,1,0:T(8,128)(2,1)S(1)} %slice.16), channel_id=1, source_target_pairs={{0,8},{8,16},{16,24},{1,9},{9,17},{17,25},{2,10},{10,18},{18,26},{... | collective-permute-start | bytes 1081352 | tf_op jit(solution)/shard_map/ppermute | solution.py:594
  24.2 11.2 %collective-permute-start.9 = (bf16[1,80,1024]{2,1,0:T(8,128)(2,1)S(1)}, bf16[1,80,1024]{2,1,0:T(8,128)(2,1)S(1)}, u32[]{:S(2)}, u32[]{:S(2)}) collective-permute-start(bf16[1,80,1024]{2,1,0:T(8,128)(2,1)S(1)} %slice.14), channel_id=1, source_target_pairs={{4,8},{12,16},{20,24},{5,9},{13,17},{21,25},{6,10},{14,18},{22,26}... | collective-permute-start | bytes 491528 | tf_op jit(solution)/shard_map/ppermute | solution.py:603

commit v5 on v4

--- a/solution.py
+++ b/solution.py
@@ -448,7 +448,7 @@
 
 
 def last_kernel(
-    rows, cos_ref, sin_ref, bias_ref, level_ref, mean_ref, q_ref, key_ref, swapped_value,
+    rows, bias_ref, level_ref, mean_ref, q_ref, key_ref, swapped_value,
     passed_value, direct_value, out_ref, held, sem, *refs,
 ):
     work = split_work(refs)
@@ -459,7 +459,7 @@
     for group in range(KEY_VALUE_HEADS // HEADS_PER_STEP):
         for part in range(HEADS_PER_STEP):
             lanes = pl.ds((group * HEADS_PER_STEP + part) * HEAD_SIZE, HEAD_SIZE)
-            rotate_rows(k_parts[part], 0, key_ref, lanes, cos_ref, sin_ref)
+            k_parts[part][...] = key_ref[0, :, lanes]
             start = 0
             for arrived in (passed_value, direct_value):
                 span = pl.ds(start, arrived.shape[1])
@@ -486,9 +486,27 @@
     return ref.at[:, :, lanes] if len(ref.shape) == 3 else ref.at[:, lanes]
 
 
-def attend_last(cosine, signed_sine, bias, level, mean, query, arrived):
+def turn_kernel(cos_ref, sin_ref, key_ref, out_ref):
+    for start in range(0, key_ref.shape[2], HEAD_SIZE):
+        lanes = pl.ds(start, HEAD_SIZE)
+        rotate_rows(out_ref.at[0, :, lanes], 0, key_ref, lanes, cos_ref, sin_ref)
+
+
+def turn(cosine, signed_sine, key):
+    return pl.pallas_call(
+        turn_kernel,
+        in_specs=[pl.BlockSpec(memory_space=pltpu.VMEM)] * 3,
+        out_specs=pl.BlockSpec(memory_space=pltpu.VMEM),
+        out_shape=jax.ShapeDtypeStruct(key.shape, key.dtype),
+        compiler_params=pltpu.CompilerParams(vmem_limit_bytes=vmem_bytes(key.shape[1])),
+        cost_estimate=cost(0),
+        name="turn",
+    )(cosine, signed_sine, key)
+
+
+def attend_last(bias, level, mean, query, arrived):
     rows = query.shape[1]
-    operands = [cosine, signed_sine, bias, level, mean, query, *arrived]
+    operands = [bias, level, mean, query, *arrived]
     return pl.pallas_call(
         lambda *refs: last_kernel(rows, *refs),
         in_specs=[pl.BlockSpec(memory_space=pltpu.VMEM)] * len(operands),
@@ -608,8 +626,8 @@
         pages=gather_pages(table, [(0, 0, own_shard), *shards]),
     )
     result = attend_last(
-        cos_last, sin_last, last_bias, level, mean, query,
-        [far_key, swapped_value, passed_value, direct_value],
+        last_bias, level, mean, query,
+        [turn(cos_last, sin_last, far_key), swapped_value, passed_value, direct_value],
     )
     return (result, key)
 

time: 40 us -> 39.5 us (0.988)
  Pallas kernels: 17.9 us -> 17.4 us
    ppermute x1, waiting for transfers between devices: 0.75 us -> 2.08 us  [per_device(): far_key = lax.ppermute(to_swap, 'blk', swap)]
    ppermute x1, waiting for transfers between devices: 1.32 us -> 0.01 us  [per_device(): lax.ppermute(swapped_value[:, :split], 'blk', [(j, j + 2) for j in range(...]
    pallas_call x1, Pallas kernels: 3.6 us -> 2.83 us  [attend_last(): pl.pallas_call(lambda *refs: last_kernel(rows, *refs), in_specs=[pl.Block...]
  transfers between devices with their start and end apart: 10 -> 10, of which waited for: 4 -> 3; matrix products, arithmetic and copies ran while one was open for 4% -> 4% of each run, Pallas kernels for 36% -> 37%
where the time goes in v5:
time: 39.5 us; the launch traced here: 39.3 us
  Pallas kernels  17.4 us (44%)
  starting transfers between devices  16.1 us (41%)
  waiting for transfers between devices  3.32 us (8%)
  local copies, waits for them, and re-layouts  0.86 us (2%)
  between operations  0.83 us (2%)
  other arithmetic  0.82 us (2%)
    ppermute x2, starting transfers between devices, shifted(): lax.ppermute(value, 'blk', [(source, source + steps) for source in range(...  6.96 us
    pallas_call x1, Pallas kernels, attend_far(): pl.pallas_call(kernel, grid=(KEY_VALUE_HEADS // HEADS_PER_STEP,), in_spec...  5.25 us
    ppermute x1, starting transfers between devices, per_device(): lax.ppermute(swapped_value[:, :split], 'blk', [(j, j + 2) for j in range(...  3.48 us
    pallas_call x1, Pallas kernels, attend_last(): pl.pallas_call(lambda *refs: last_kernel(rows, *refs), in_specs=[pl.Block...  2.83 us
    pallas_call x1, Pallas kernels, attend_own(): pl.pallas_call(lambda *refs: own_kernel(rows, *refs), grid=(KEY_VALUE_HEA...  2.79 us
    pallas_call x1, Pallas kernels, gather_pages(): pl.pallas_call(lambda *refs: gather_kernel(pool_rows, places, *refs), in_...  2.36 us
    ppermute x4, starting transfers between devices, swapped(): return lax.ppermute(shard, 'batch', [(c, c ^ bit) for c in range(count)])  2.23 us
    ppermute x1, waiting for transfers between devices, per_device(): far_key = lax.ppermute(to_swap, 'blk', swap)  2.08 us
  transfers between devices with their start and end apart: 10, of which 3 were waited for; matrix products, arithmetic and copies ran while one was open for 4% of the time, Pallas kernels for 37%

profile of v5, /device:TPU:8, one launch (start us, length us, event | category | flops | bytes accessed | tf_op | source)
XLA Modules:
  0.0 39.3 jit_solution(2119183365895288533)
XLA Ops:
  0.6 3.5 %collective-permute-start.2 = (bf16[1,256,1024]{2,1,0:T(8,128)(2,1)}, bf16[1,256,1024]{2,1,0:T(8,128)(2,1)S(1)}, u32[]{:S(2)}, u32[]{:S(2)}) collective-permute-start(bf16[1,256,1024]{2,1,0:T(8,128)(2,1)} %refs_3_.1), channel_id=1, source_target_pairs={{0,8},{4,12},{8,16},{12,20},{16,24},{20,28},{1,9},{5,13},{9,17},{1... | collective-permute-start | bytes 1572872 | tf_op jit(solution)/shard_map/ppermute | solution.py:45
  4.1 0.1 collective-permute-start
  4.2 1.6 %collective-permute-start.1 = (bf16[8,16,2048]{2,1,0:T(8,128)(2,1)}, bf16[8,16,2048]{2,1,0:T(8,128)(2,1)S(1)}, u32[]{:S(2)}, u32[]{:S(2)}) collective-permute-start(bf16[8,16,2048]{2,1,0:T(8,128)(2,1)} %refs_5_.1), channel_id=1, source_target_pairs={{0,2},{1,3},{2,0},{3,1},{4,6},{5,7},{6,4},{7,5},{8,10},{9,11},{10,... | collective-permute-start | bytes 1572872 | tf_op jit(solution)/shard_map/ppermute | solution.py:573
  5.8 1.5 %collective-permute-start.3 = (bf16[1,256,1024]{2,1,0:T(8,128)(2,1)}, bf16[1,256,1024]{2,1,0:T(8,128)(2,1)S(1)}, u32[]{:S(2)}, u32[]{:S(2)}) collective-permute-start(bf16[1,256,1024]{2,1,0:T(8,128)(2,1)} %refs_4_.1), channel_id=1, source_target_pairs={{0,4},{4,0},{8,12},{12,8},{16,20},{20,16},{24,28},{28,24},{1,5},{5... | collective-permute-start | bytes 1572872 | tf_op jit(solution)/shard_map/ppermute | solution.py:601
  7.3 3.5 %collective-permute-start.6 = (bf16[1,256,1024]{2,1,0:T(8,128)(2,1)}, bf16[1,256,1024]{2,1,0:T(8,128)(2,1)S(1)}, u32[]{:S(2)}, u32[]{:S(2)}) collective-permute-start(bf16[1,256,1024]{2,1,0:T(8,128)(2,1)} %refs_4_.1), channel_id=1, source_target_pairs={{0,8},{4,12},{8,16},{12,20},{16,24},{20,28},{1,9},{5,13},{9,17},{1... | collective-permute-start | bytes 1572872 | tf_op jit(solution)/shard_map/ppermute | solution.py:45
  10.8 0.8 %reshape.15 = s32[56]{0:T(128)S(1)} reshape(s32[4,2,7]{2,1,0:T(2,128)} %bitcast.3) | data formatting | bytes 448 | tf_op jit(solution)/shard_map/reshape | solution.py:602
  11.5 0.8 %pad_add_fusion.refs_0_ = s32[65]{0:T(128)S(1)} fusion(s32[56]{0:T(128)S(1)} %reshape.15, s32[2]{0:T(128)} %bitcast.4, s32[7]{0:T(128)} %bitcast.5), kind=kLoop, calls=%fused_computation.1 | loop fusion | flops 130 | bytes 520 | tf_op jit(solution)/shard_map/concatenate | solution.py:602
  12.3 0.0 copy-start
  12.3 0.0 copy-start.1
  12.3 0.0 copy-start.2
  12.3 0.0 copy-start.3
  12.3 2.0 %tables.1 = (s32[14]{0:T(128)S(1)}, f32[256,128]{1,0:T(8,128)S(1)}, f32[256,128]{1,0:T(8,128)S(1)}, f32[256,128]{1,0:T(8,128)S(1)}, f32[256,128]{1,0:T(8,128)S(1...) custom-call(s32[65]{0:T(128)S(1)} %pad_add_fusion.refs_0_), custom_call_target="tpu_custom_call" | custom-call | flops 2000000000 | tf_op jit(solution)/shard_map/tables/pallas_call | solution.py:159
  14.4 0.0 copy-done
  14.4 0.0 copy-done.1
  14.4 0.0 copy-done.2
  14.4 0.0 copy-done.3
  14.4 1.8 %prepare.1 = (bf16[1,256,2048]{2,1,0:T(8,128)(2,1)S(1)}, bf16[1,256,1024]{2,1,0:T(8,128)(2,1)}, bf16[1,256,1024]{2,1,0:T(8,128)(2,1)S(1)}, bf16[1,256,1024]{2,1,0:T(8,128)(2,1)S(1)}, bf16[8,16,2048]{2,1,0:T(8,128)(2,1)S(1)}) custom-call(f32[256,128]{1,0:T(8,128)S(1)} %get-tuple-element.33.refs_0_, f32[256,128]{1,0:T(8,128)S(1)} %get-tuple-element.34.refs_1_, ...), custom_call_target="tpu_custom_call" | custom-call | tf_op jit(solution)/shard_map/prepare/pallas_call | solution.py:199
  16.2 2.8 %own.1 = (f32[256,2048]{1,0:T(8,128)S(1)}, f32[256,128]{1,0:T(8,128)S(1)}) custom-call(f32[256,256]{1,0:T(8,128)S(1)} %get-tuple-element.32.refs_0_, bf16[1,256,2048]{2,1,0:T(8,128)(2,1)S(1)} %get-tuple-element.35.refs_1_.refs_5_.refs_3_, bf16[1,256,1024]{2,1,0:T(8,128)(2,1)S(1)} %get-tuple-element.36.refs_2_, ...), custom_call_target="tpu_custom_call" | custom-call | tf_op jit(solution)/shard_map/own/pallas_call | solution.py:302
  19.0 0.0 collective-permute-done.2.refs_8_
  19.0 0.1 broadcast_select_fusion
  19.1 0.6 %collective-permute-start.7 = (bf16[1,256,1024]{2,1,0:T(8,128)(2,1)S(1)}, bf16[1,256,1024]{2,1,0:T(8,128)(2,1)S(1)}, u32[]{:S(2)}, u32[]{:S(2)}) collective-permute-start(bf16[1,256,1024]{2,1,0:T(8,128)(2,1)S(1)} %broadcast_select_fusion), channel_id=1, source_target_pairs={{0,4},{4,0},{8,12},{12,8},{16,20},{20,16},{24,28},{28,24},{1,5},{5... | collective-permute-start | bytes 1572872 | tf_op jit(solution)/shard_map/ppermute | solution.py:610
  19.7 0.3 collective-permute-done.3.refs_5_
  20.0 0.0 collective-permute-done.refs_2_
  20.0 0.0 collective-permute-done.1.refs_3_
  20.0 0.1 collective-permute-start.4
  20.1 0.5 %collective-permute-start.5 = (bf16[4,16,2048]{2,1,0:T(8,128)(2,1)S(1)}, bf16[4,16,2048]{2,1,0:T(8,128)(2,1)S(1)}, u32[]{:S(2)}, u32[]{:S(2)}) collective-permute-start(bf16[4,16,2048]{2,1,0:T(8,128)(2,1)S(1)} %get-tuple-element.54), channel_id=1, source_target_pairs={{0,1},{1,0},{2,3},{3,2},{4,5},{5,4},{6,7},{7,6},{8,9},{9,8},{10,11... | collective-permute-start | bytes 786440 | tf_op jit(solution)/shard_map/ppermute | solution.py:573
  20.6 3.5 %collective-permute-start.8 = (bf16[1,176,1024]{2,1,0:T(8,128)(2,1)S(1)}, bf16[1,176,1024]{2,1,0:T(8,128)(2,1)S(1)}, u32[]{:S(2)}, u32[]{:S(2)}) collective-permute-start(bf16[1,176,1024]{2,1,0:T(8,128)(2,1)S(1)} %slice.16), channel_id=1, source_target_pairs={{0,8},{8,16},{16,24},{1,9},{9,17},{17,25},{2,10},{10,18},{18,26},{... | collective-permute-start | bytes 1081352 | tf_op jit(solution)/shard_map/ppermute | solution.py:612
  24.2 0.0 collective-permute-done.4.refs_4_
  24.2 0.0 collective-permute-done.5.refs_5_
  24.2 1.3 %collective-permute-start.9 = (bf16[1,80,1024]{2,1,0:T(8,128)(2,1)S(1)}, bf16[1,80,1024]{2,1,0:T(8,128)(2,1)S(1)}, u32[]{:S(2)}, u32[]{:S(2)}) collective-permute-start(bf16[1,80,1024]{2,1,0:T(8,128)(2,1)S(1)} %slice.14), channel_id=1, source_target_pairs={{4,8},{12,16},{20,24},{5,9},{13,17},{21,25},{6,10},{14,18},{22,26}... | collective-permute-start | bytes 491528 | tf_op jit(solution)/shard_map/ppermute | solution.py:621
  25.5 2.4 %gather.1.refs_6_.refs_7_ = bf16[14,16,2048]{2,1,0:T(8,128)(2,1)S(1)} custom-call(s32[14]{0:T(128)S(1)} %get-tuple-element.40.refs_0_, bf16[8,16,2048]{2,1,0:T(8,128)(2,1)S(1)} %get-tuple-element.41.refs_1_, bf16[8,16,2048]{2,1,0:T(8,128)(2,1)S(1)} %collective-permute-done.refs_2_, bf16[8,16,2048]{2,1,0:T(8,128)(2,1)S(1)} %collective-permute-done.1.refs_3_, ...), custom_call_target="tpu_custom_call" | custom-call | tf_op jit(solution)/shard_map/gather/pallas_call | solution.py:351
  27.8 0.9 %collective-permute-done.6.refs_9_ = bf16[1,256,1024]{2,1,0:T(8,128)(2,1)S(1)} collective-permute-done((bf16[1,256,1024]{2,1,0:T(8,128)(2,1)}, bf16[1,256,1024]{2,1,0:T(8,128)(2,1)S(1)}, u32[]{:S(2)}, u32[]{:S(2)}) %collective-permute-start.6) | collective-permute-done | bytes 524320 | tf_op jit(solution)/shard_map/ppermute | solution.py:45
  28.8 5.2 %far.1 = (f32[256,2048]{1,0:T(8,128)S(1)}, f32[256,128]{1,0:T(8,128)S(1)}) custom-call(f32[256,128]{1,0:T(8,128)S(1)} %get-tuple-element.29.refs_0_, f32[256,128]{1,0:T(8,128)S(1)} %get-tuple-element.30.refs_1_, f32[256,512]{1,0:T(8,128)S(1)} %get-tuple-element.31.refs_2_, f32[256,128]{1,0:T(8,128)S(1)} %get-tuple-element.38.refs_3_, ...), custom_call_target="tpu_custom_call" | custom-call | tf_op jit(solution)/shard_map/far/pallas_call | solution.py:556
  34.0 2.1 %collective-permute-done.7.key_ref = bf16[1,256,1024]{2,1,0:T(8,128)(2,1)S(1)} collective-permute-done((bf16[1,256,1024]{2,1,0:T(8,128)(2,1)S(1)}, bf16[1,256,1024]{2,1,0:T(8,128)(2,1)S(1)}, u32[]{:S(2)}, u32[]{:S(2)}) %collective-permute-start.7) | collective-permute-done | bytes 524320 | tf_op jit(solution)/shard_map/ppermute | solution.py:610
  36.1 0.3 turn.1.refs_4_
  36.4 0.0 collective-permute-done.8.refs_6_
  36.4 0.0 collective-permute-done.9.refs_7_
  36.4 2.8 %last.1 = bf16[1,256,2048]{2,1,0:T(8,128)(2,1)} custom-call(f32[256,256]{1,0:T(8,128)S(1)} %get-tuple-element.28.refs_0_, f32[256,128]{1,0:T(8,128)S(1)} %get-tuple-element.48.refs_1_, f32[256,2048]{1,0:T(8,128)S(1)} %get-tuple-element.49.refs_2_, bf16[1,256,2048]{2,1,0:T(8,128)(2,1)S(1)} %get-tuple-element.35.refs_1_.refs_5_.refs_3_, ...), custom_call_target="tpu_custom_call" | custom-call | tf_op jit(solution)/shard_map/last/pallas_call | solution.py:510
  (3 shorter events, 0.1 us)
Async XLA Ops:
  0.6 18.4 %collective-permute-start.2 = (bf16[1,256,1024]{2,1,0:T(8,128)(2,1)}, bf16[1,256,1024]{2,1,0:T(8,128)(2,1)S(1)}, u32[]{:S(2)}, u32[]{:S(2)}) collective-permute-start(bf16[1,256,1024]{2,1,0:T(8,128)(2,1)} %refs_3_.1), channel_id=1, source_target_pairs={{0,8},{4,12},{8,16},{12,20},{16,24},{20,28},{1,9},{5,13},{9,17},{1... | collective-permute-start | bytes 1572872 | tf_op jit(solution)/shard_map/ppermute | solution.py:45
  4.1 15.9 %collective-permute-start = (bf16[8,16,2048]{2,1,0:T(8,128)(2,1)}, bf16[8,16,2048]{2,1,0:T(8,128)(2,1)S(1)}, u32[]{:S(2)}, u32[]{:S(2)}) collective-permute-start(bf16[8,16,2048]{2,1,0:T(8,128)(2,1)} %refs_5_.1), channel_id=1, source_target_pairs={{0,1},{1,0},{2,3},{3,2},{4,5},{5,4},{6,7},{7,6},{8,9},{9,8},{10,11... | collective-permute-start | bytes 1572872 | tf_op jit(solution)/shard_map/ppermute | solution.py:573
  4.2 15.8 %collective-permute-start.1 = (bf16[8,16,2048]{2,1,0:T(8,128)(2,1)}, bf16[8,16,2048]{2,1,0:T(8,128)(2,1)S(1)}, u32[]{:S(2)}, u32[]{:S(2)}) collective-permute-start(bf16[8,16,2048]{2,1,0:T(8,128)(2,1)} %refs_5_.1), channel_id=1, source_target_pairs={{0,2},{1,3},{2,0},{3,1},{4,6},{5,7},{6,4},{7,5},{8,10},{9,11},{10,... | collective-permute-start | bytes 1572872 | tf_op jit(solution)/shard_map/ppermute | solution.py:573
  5.8 14.2 %collective-permute-start.3 = (bf16[1,256,1024]{2,1,0:T(8,128)(2,1)}, bf16[1,256,1024]{2,1,0:T(8,128)(2,1)S(1)}, u32[]{:S(2)}, u32[]{:S(2)}) collective-permute-start(bf16[1,256,1024]{2,1,0:T(8,128)(2,1)} %refs_4_.1), channel_id=1, source_target_pairs={{0,4},{4,0},{8,12},{12,8},{16,20},{20,16},{24,28},{28,24},{1,5},{5... | collective-permute-start | bytes 1572872 | tf_op jit(solution)/shard_map/ppermute | solution.py:601
  7.3 21.5 %collective-permute-start.6 = (bf16[1,256,1024]{2,1,0:T(8,128)(2,1)}, bf16[1,256,1024]{2,1,0:T(8,128)(2,1)S(1)}, u32[]{:S(2)}, u32[]{:S(2)}) collective-permute-start(bf16[1,256,1024]{2,1,0:T(8,128)(2,1)} %refs_4_.1), channel_id=1, source_target_pairs={{0,8},{4,12},{8,16},{12,20},{16,24},{20,28},{1,9},{5,13},{9,17},{1... | collective-permute-start | bytes 1572872 | tf_op jit(solution)/shard_map/ppermute | solution.py:45
  12.3 2.1 %copy-start = (bf16[1,256,1024]{2,1,0:T(8,128)(2,1)S(1)}, bf16[1,256,1024]{2,1,0:T(8,128)(2,1)}, u32[]{:S(2)}) copy-start(bf16[1,256,1024]{2,1,0:T(8,128)(2,1)} %refs_3_.1) | copy-start | bytes 1572868
  12.3 2.1 %copy-start.1 = (bf16[1,256,2048]{2,1,0:T(8,128)(2,1)S(1)}, bf16[1,256,2048]{2,1,0:T(8,128)(2,1)}, u32[]{:S(2)}) copy-start(bf16[1,256,2048]{2,1,0:T(8,128)(2,1)} %refs_2_.1) | copy-start | bytes 3145732
  12.3 2.1 %copy-start.2 = (bf16[1,256,1024]{2,1,0:T(8,128)(2,1)S(1)}, bf16[1,256,1024]{2,1,0:T(8,128)(2,1)}, u32[]{:S(2)}) copy-start(bf16[1,256,1024]{2,1,0:T(8,128)(2,1)} %refs_4_.1) | copy-start | bytes 1572868
  12.3 2.1 %copy-start.3 = (bf16[8,16,2048]{2,1,0:T(8,128)(2,1)S(1)}, bf16[8,16,2048]{2,1,0:T(8,128)(2,1)}, u32[]{:S(2)}) copy-start(bf16[8,16,2048]{2,1,0:T(8,128)(2,1)} %refs_5_.1) | copy-start | bytes 1572868
  19.1 17.0 %collective-permute-start.7 = (bf16[1,256,1024]{2,1,0:T(8,128)(2,1)S(1)}, bf16[1,256,1024]{2,1,0:T(8,128)(2,1)S(1)}, u32[]{:S(2)}, u32[]{:S(2)}) collective-permute-start(bf16[1,256,1024]{2,1,0:T(8,128)(2,1)S(1)} %broadcast_select_fusion), channel_id=1, source_target_pairs={{0,4},{4,0},{8,12},{12,8},{16,20},{20,16},{24,28},{28,24},{1,5},{5... | collective-permute-start | bytes 1572872 | tf_op jit(solution)/shard_map/ppermute | solution.py:610
  20.0 4.1 %collective-permute-start.4 = (bf16[4,16,2048]{2,1,0:T(8,128)(2,1)S(1)}, bf16[4,16,2048]{2,1,0:T(8,128)(2,1)S(1)}, u32[]{:S(2)}, u32[]{:S(2)}) collective-permute-start(bf16[4,16,2048]{2,1,0:T(8,128)(2,1)S(1)} %get-tuple-element.55), channel_id=1, source_target_pairs={{0,1},{1,0},{2,3},{3,2},{4,5},{5,4},{6,7},{7,6},{8,9},{9,8},{10,11... | collective-permute-start | bytes 786440 | tf_op jit(solution)/shard_map/ppermute | solution.py:573
  20.1 4.1 %collective-permute-start.5 = (bf16[4,16,2048]{2,1,0:T(8,128)(2,1)S(1)}, bf16[4,16,2048]{2,1,0:T(8,128)(2,1)S(1)}, u32[]{:S(2)}, u32[]{:S(2)}) collective-permute-start(bf16[4,16,2048]{2,1,0:T(8,128)(2,1)S(1)} %get-tuple-element.54), channel_id=1, source_target_pairs={{0,1},{1,0},{2,3},{3,2},{4,5},{5,4},{6,7},{7,6},{8,9},{9,8},{10,11... | collective-permute-start | bytes 786440 | tf_op jit(solution)/shard_map/ppermute | solution.py:573
  20.6 15.8 %collective-permute-start.8 = (bf16[1,176,1024]{2,1,0:T(8,128)(2,1)S(1)}, bf16[1,176,1024]{2,1,0:T(8,128)(2,1)S(1)}, u32[]{:S(2)}, u32[]{:S(2)}) collective-permute-start(bf16[1,176,1024]{2,1,0:T(8,128)(2,1)S(1)} %slice.16), channel_id=1, source_target_pairs={{0,8},{8,16},{16,24},{1,9},{9,17},{17,25},{2,10},{10,18},{18,26},{... | collective-permute-start | bytes 1081352 | tf_op jit(solution)/shard_map/ppermute | solution.py:612
  24.2 12.3 %collective-permute-start.9 = (bf16[1,80,1024]{2,1,0:T(8,128)(2,1)S(1)}, bf16[1,80,1024]{2,1,0:T(8,128)(2,1)S(1)}, u32[]{:S(2)}, u32[]{:S(2)}) collective-permute-start(bf16[1,80,1024]{2,1,0:T(8,128)(2,1)S(1)} %slice.14), channel_id=1, source_target_pairs={{4,8},{12,16},{20,24},{5,9},{13,17},{21,25},{6,10},{14,18},{22,26}... | collective-permute-start | bytes 491528 | tf_op jit(solution)/shard_map/ppermute | solution.py:621
